TPU v7x, 256 devices: a whole 4x4x8 slice. The times are simulated.
256 devices in a mesh: engine: 32 (over x, y, core), tp: 8 (over z).
Axes of the slice: x: 4, y: 4, z: 8, core: 2. Of those that a mesh axis runs over, the one named last changes fastest.
Arguments:
- outgoing: bfloat16 [384, 32, 4096], P('engine'), may hold values from -24 to 24
- span_target: int32 [32, 12], replicated, may hold values from 0 to 31, as said below
- span_row: int32 [32, 12], replicated, may hold values from 0 to 7
- span_block: int32 [32, 12], replicated, may hold values from 0 to 63
- span_tokens: int32 [32, 12], replicated, may hold values from 1 to 32
- norm_gain: float32 [4096], replicated, may hold values from 0.3 to 3
- key_weight: bfloat16 [4096, 4096], P(None, 'tp'), may hold values from -0.09375 to 0.09375
- value_weight: bfloat16 [4096, 4096], P(None, 'tp'), may hold values from -0.09375 to 0.09375
- fresh_states: bfloat16 [2, 256, 4096], P(None, ('engine', 'tp')), may hold values from -24 to 24
- queries: bfloat16 [2, 256, 4096], P(None, 'engine', 'tp'), may hold values from -16 to 16
- res_keys: bfloat16 [256, 64, 4096], P('engine', None, 'tp'), may hold values from -16 to 16
- res_values: bfloat16 [256, 64, 4096], P('engine', None, 'tp'), may hold values from -6 to 6
- res_len: int32 [256], P('engine'), may hold values from 2 to 64
Outputs:
- attended: bfloat16 [2, 256, 4096], P(None, 'engine', 'tp')
Inputs may be any that keep to these rules, and one draw needn't show every extreme that they name: `span_target`: each engine sends its 12 spans to 12 different engines, never to itself; an engine receives at most 24 spans, and some engine receives exactly 24.
All inputs are finite; a program needn't handle non-finite values.
Results may differ from a plain program's by a relative error of at most 0.0071.
Values may be sent and summed in bfloat16 or wider, within the bound.
A program may use at most 64 MiB of HBM per device.

v0:
```python
import math

import jax
import jax.numpy as jnp
from jax import lax
from jax.sharding import PartitionSpec as P

HD = 128
CTX = 2048


rope_base = 1000000.0
norm_eps = 1e-06


def rotate(projected, positions):
    count, full_width = projected.shape
    half_size = HD // 2
    per_head = projected.reshape(count, full_width // HD, HD)
    frequency = jnp.exp(
        jnp.arange(half_size, dtype=jnp.float32) * (-2.0 * math.log(rope_base) / HD)
    )
    angles = positions.astype(jnp.float32)[:, None] * frequency[None, :]
    cosine_table = jnp.cos(angles)[:, None, :]
    sine_table = jnp.sin(angles)[:, None, :]
    lower_half = per_head[..., :half_size]
    upper_half = per_head[..., half_size:]
    turned = jnp.concatenate(
        [
            lower_half * cosine_table - upper_half * sine_table,
            upper_half * cosine_table + lower_half * sine_table,
        ],
        axis=-1,
    )
    return turned.reshape(count, full_width)


def normalize(states, norm_gain):
    widened = states.astype(jnp.float32)
    factor = lax.rsqrt(jnp.mean(widened * widened, axis=-1, keepdims=True) + norm_eps)
    return (widened * factor * norm_gain).astype(jnp.bfloat16)


def project(normed, key_weight, value_weight, positions):
    key_raw = jnp.dot(normed, key_weight, preferred_element_type=jnp.float32)
    values_out = jnp.dot(normed, value_weight, preferred_element_type=jnp.float32).astype(
        jnp.bfloat16
    )
    return (rotate(key_raw, positions).astype(jnp.bfloat16), values_out)


def attend(
    queries,
    res_keys,
    res_values,
    res_len,
    slot_keys,
    slot_values,
    slot_row,
    slot_tokens,
    fresh_keys,
    fresh_values,
):
    step_count, row_count, full_width = queries.shape
    head_count = full_width // HD
    slot_count, slot_size = (slot_keys.shape[0], slot_keys.shape[1])
    resident = res_keys.shape[1]
    moved_count = slot_count * slot_size
    turned = queries.reshape(step_count, row_count, head_count, HD)
    near_keys = res_keys.reshape(row_count, resident, head_count, HD)
    moved_keys = slot_keys.reshape(moved_count, head_count, HD)
    newest_keys = fresh_keys.reshape(step_count, row_count, head_count, HD)
    score_near = jnp.einsum(
        "srhd,rjhd->srhj", turned, near_keys, preferred_element_type=jnp.float32
    )
    score_moved = jnp.einsum(
        "srhd,khd->srhk", turned, moved_keys, preferred_element_type=jnp.float32
    )
    score_newest = jnp.einsum(
        "srhd,urhd->srhu", turned, newest_keys, preferred_element_type=jnp.float32
    )
    live_near = jnp.arange(resident, dtype=jnp.int32)[None, :] < res_len[:, None]
    row_match = slot_row[None, :, None] == jnp.arange(row_count, dtype=jnp.int32)[:, None, None]
    token_live = jnp.arange(slot_size, dtype=jnp.int32)[None, None, :] < slot_tokens[None, :, None]
    live_moved = (row_match & token_live).reshape(row_count, moved_count)
    live_newest = jnp.arange(step_count)[None, :] <= jnp.arange(step_count)[:, None]
    scores = jnp.concatenate(
        [
            jnp.where(live_near[None, :, None, :], score_near, -jnp.inf),
            jnp.where(live_moved[None, :, None, :], score_moved, -jnp.inf),
            jnp.where(live_newest[:, None, None, :], score_newest, -jnp.inf),
        ],
        axis=-1,
    ) * (1.0 / math.sqrt(HD))
    row_peak = jnp.max(scores, axis=-1, keepdims=True)
    expo = jnp.exp(scores - row_peak)
    weights = (expo / jnp.sum(expo, axis=-1, keepdims=True)).astype(jnp.bfloat16)
    w_near = weights[..., :resident]
    w_moved = weights[..., resident : resident + moved_count]
    w_newest = weights[..., resident + moved_count :]
    result = jnp.einsum(
        "srhj,rjhd->srhd",
        w_near,
        res_values.reshape(row_count, resident, head_count, HD),
        preferred_element_type=jnp.float32,
    )
    result = result + jnp.einsum(
        "srhk,khd->srhd",
        w_moved,
        slot_values.reshape(moved_count, head_count, HD),
        preferred_element_type=jnp.float32,
    )
    result = result + jnp.einsum(
        "srhu,urhd->srhd",
        w_newest,
        fresh_values.reshape(step_count, row_count, head_count, HD),
        preferred_element_type=jnp.float32,
    )
    return result.reshape(step_count, row_count, full_width).astype(jnp.bfloat16)


def per_device(
    outgoing,
    span_target,
    span_row,
    span_block,
    span_tokens,
    norm_gain,
    key_weight,
    value_weight,
    fresh_states,
    queries,
    res_keys,
    res_values,
    res_len,
):
    engines = lax.axis_size("engine")
    engine_id = lax.axis_index("engine")
    send_count, slot_size, model_width = outgoing.shape
    local_width = key_weight.shape[1]
    offsets = jnp.arange(slot_size, dtype=jnp.int32)
    engine_ids = jnp.arange(engines, dtype=jnp.int32)
    my_targets = lax.dynamic_index_in_dim(span_target, engine_id, 0, keepdims=False)
    my_blocks = lax.dynamic_index_in_dim(span_block, engine_id, 0, keepdims=False)
    routing = (engine_ids[:, None] == my_targets[None, :]).astype(jnp.bfloat16)
    incoming = (span_target == engine_id).astype(jnp.int32)
    arriving = jnp.sum(incoming, axis=1)
    from_row = jnp.sum(incoming * span_row, axis=1)
    from_tokens = jnp.sum(incoming * span_tokens, axis=1)
    fresh_all = lax.all_gather(fresh_states, "tp", axis=1, tiled=True)
    step_count, row_count = (fresh_all.shape[0], fresh_all.shape[1])
    fresh_positions = CTX + jnp.repeat(jnp.arange(step_count, dtype=jnp.int32), row_count)
    fresh_keys, fresh_values = project(
        normalize(fresh_all.reshape(step_count * row_count, model_width), norm_gain),
        key_weight,
        value_weight,
        fresh_positions,
    )
    positions = (my_blocks[:, None] * slot_size + offsets[None, :]).reshape(-1)
    built_keys, built_values = project(
        normalize(outgoing.reshape(send_count * slot_size, model_width), norm_gain),
        key_weight,
        value_weight,
        positions,
    )
    packed = jnp.concatenate([built_keys, built_values], axis=1).reshape(
        send_count, slot_size, 2 * local_width
    )
    outbox = jnp.einsum("ek,kcf->ecf", routing, packed, preferred_element_type=jnp.float32).astype(
        jnp.bfloat16
    )
    arrived = lax.all_to_all(outbox, "engine", split_axis=0, concat_axis=0, tiled=True)
    slot_keys = arrived[:, :, :local_width]
    slot_values = arrived[:, :, local_width:]
    slot_row = jnp.where(arriving > 0, from_row, -1)
    return attend(
        queries,
        res_keys,
        res_values,
        res_len,
        slot_keys,
        slot_values,
        slot_row,
        from_tokens,
        fresh_keys.reshape(step_count, row_count, local_width),
        fresh_values.reshape(step_count, row_count, local_width),
    )


def solution(mesh):
    in_specs = (
        P("engine", None, None),
        P(),
        P(),
        P(),
        P(),
        P(),
        P(None, "tp"),
        P(None, "tp"),
        P(None, ("engine", "tp"), None),
        P(None, "engine", "tp"),
        P("engine", None, "tp"),
        P("engine", None, "tp"),
        P("engine"),
    )
    out_specs = P(None, "engine", "tp")
    return jax.shard_map(
        per_device, mesh=mesh, in_specs=in_specs, out_specs=out_specs, check_vma=False
    )
```

profile of v0, /device:TPU:2, one launch (start us, length us, event | category | flops | bytes accessed | tf_op | source)
XLA Modules:
  0.0 74.1 jit_solution(10511673565585492569)
XLA Ops:
  0.0 0.0 copy-start
  0.0 1.0 %multiply_reduce_fusion.2 = (s32[12]{0:T(128)S(1)}, s32[12]{0:T(128)S(1)}) fusion(s32[32,12]{0,1:T(8,128)} %param.16, s32[]{:T(128)S(6)} %select_n.31, s32[32,12]{0,1:T(8,128)} %param.14), kind=kLoop, calls=%fused_computation.75 | loop fusion | flops 12 | bytes 196 | tf_op jit(solution)/shard_map/mul | solution.py:159
  1.0 0.1 add_convert_fusion.2
  1.0 0.1 convert_element_type.104
  1.1 6.4 %copy.74 = bf16[512,4096]{1,0:T(8,128)(2,1)} copy(bf16[512,4096]{0,1:T(8,128)(2,1)} %bitcast.98) | data formatting | bytes 8388608 | tf_op jit(solution)/shard_map/dot_general | solution.py:45
  7.6 2.6 %multiply_reduce_fusion = f32[12,32]{1,0:T(8,128)S(1)} fusion(bf16[12,32,4096]{2,1,0:T(8,128)(2,1)} %param.13), kind=kLoop, calls=%fused_computation.5 | loop fusion | flops 4718208 | bytes 3147264 | tf_op jit(solution)/shard_map/reduce_sum | solution.py:40
  10.1 0.1 rsqrt.25
  10.2 0.0 copy-done.5
  10.2 3.0 %multiply_convert_fusion = bf16[12,32,4096]{2,1,0:T(8,128)(2,1)S(1)} fusion(f32[4096]{0:T(1024)S(1)} %copy-done.5, f32[12,32]{1,0:T(8,128)S(1)} %add_rsqrt_fusion, bf16[12,32,4096]{2,1,0:T(8,128)(2,1)} %param.13), kind=kLoop, calls=%fused_computation.4 | loop fusion | flops 6291456 | bytes 6309376 | tf_op jit(solution)/shard_map/convert_element_type | solution.py:41
  13.3 0.4 multiply_cosine_fusion
  13.7 0.0 copy-done.1
  13.7 2.3 %fusion.51 = f32[384,4,128]{0,2,1:T(8,128)S(1)} fusion(bf16[384,4096,1]{1,0,2:T(8,128)(2,1)S(1)} %bitcast.99, bf16[4,128,4096]{2,1,0:T(8,128)(2,1)S(1)} %bitcast.96), kind=kOutput, calls=%fused_computation.96 | convolution fusion | flops 1610612736 | bytes 8126464 | tf_op jit(solution)/shard_map/dot_general | solution.py:45
  16.1 0.1 subtract_convert_fusion
  16.2 0.2 copy.56
  16.4 0.0 copy-start.2
  16.4 3.0 %fusion.2 = bf16[384,4096]{1,0:T(8,128)(2,1)S(1)} fusion(f32[4096]{0:T(1024)S(1)} %copy-done.5, f32[384]{0:T(512)S(1)} %rsqrt.25, bf16[12,32,4096]{2,1,0:T(8,128)(2,1)} %param.13), kind=kLoop, calls=%fused_computation.3 | loop fusion | flops 6291456 | bytes 6309376 | tf_op jit(solution)/shard_map/convert_element_type | solution.py:41
  19.5 0.1 copy-done.2
  19.6 1.8 %convolution_convert_fusion.1 = bf16[384,512]{1,0:T(8,128)(2,1)S(1)} fusion(bf16[384,4096]{1,0:T(8,128)(2,1)S(1)} %fusion.2, bf16[4096,512]{1,0:T(8,128)(2,1)S(1)} %copy-done.2), kind=kOutput, calls=%fused_computation.9 | convolution fusion | flops 1610809344 | bytes 7733248 | tf_op jit(solution)/shard_map/dot_general | solution.py:46
  21.4 0.1 pad_maximum_fusion
  21.4 0.8 %convolution_convert_fusion = bf16[32,32,1024]{2,0,1:T(8,128)(2,1)S(1)} fusion(bf16[12,32,1024]{2,1,0:T(8,128)(2,1)S(1)} %bitcast.97, s32[12]{0:T(128)S(1)} %get-tuple-element.21), kind=kOutput, calls=%fused_computation.8 | convolution fusion | flops 26214784 | bytes 2883632 | tf_op jit(solution)/shard_map/ek,kcf->ecf/dot_general | solution.py:169
  22.3 0.0 copy-start.6
  22.3 0.0 copy-start.8
  22.3 0.0 copy-start.9
  22.3 0.0 copy-start.7
  22.3 0.0 copy-start.12
  22.3 0.0 copy-start.10
  22.4 0.0 copy-start.11
  22.4 2.5 %copy.58 = bf16[32,32,1024]{2,1,0:T(8,128)(2,1)} copy(bf16[32,32,1024]{2,0,1:T(8,128)(2,1)S(1)} %convolution_convert_fusion) | data formatting | bytes 4194304 | tf_op jit(solution)/shard_map/convert_element_type | solution.py:169
  24.8 7.6 %all-to-all-start = ((bf16[32,32,1024]{2,1,0:T(8,128)(2,1)}), bf16[32,32,1024]{2,1,0:T(8,128)(2,1)S(1)}, u32[]{:S(2)}, u32[]{:S(2)}) async-start(bf16[32,32,1024]{2,1,0:T(8,128)(2,1)} %copy.58), calls=%async_computation | async-start | bytes 4194304 | tf_op jit(solution)/shard_map/all_to_all | solution.py:172
  32.5 0.0 copy-done.6
  32.5 0.0 copy-done.8
  32.5 0.0 copy-done.9
  32.6 0.1 broadcast_reduce_fusion
  32.7 0.0 copy-done.7
  32.7 28.4 %all_gather.3 = bf16[2,8,4096]{2,0,1:T(2,128)(2,1)S(1)} all-gather(bf16[2,1,4096]{2,0,1:T(2,128)(2,1)S(1)} %copy-done.7), channel_id=1, replica_groups=mesh['engine'=32,'tp'=8] {'tp'}, dimensions={1}, use_global_device_ids=true | all-gather | bytes 147456 | tf_op jit(solution)/shard_map/all_gather | solution.py:150
  61.1 0.2 fusion.19
  61.3 0.1 iota_compare_fusion.2
  61.4 0.4 fusion.8
  61.8 0.1 and.20
  61.9 0.1 and.21
  62.0 0.1 lt.50
  62.1 0.1 lt.48
  62.2 0.1 convert_element_type.115
  62.3 0.1 rsqrt.27
  62.4 0.1 multiply_cosine_fusion.1
  62.5 3.5 %fusion.28 = f32[16,4,128]{2,0,1:T(8,128)S(1)} fusion(bf16[4,128,4096]{2,1,0:T(8,128)(2,1)} %bitcast.95, f32[4096]{0:T(1024)S(1)} %copy-done.5, f32[2,8]{1,0:T(2,128)S(1)} %add_rsqrt_fusion.1, bf16[2,8,4096]{2,0,1:T(2,128)(2,1)S(1)} %all_gather.3), kind=kOutput, calls=%fused_computation.49 | convolution fusion | flops 67371008 | bytes 4374592 | tf_op jit(solution)/shard_map/dot_general | solution.py:45
  66.0 0.1 subtract_convert_fusion.1
  66.1 0.1 maximum_bitcast_fusion
  66.2 0.1 fusion.41
  66.4 0.7 fusion.10
  67.1 0.0 all-to-all-done
  67.1 1.7 %fusion.49 = (bf16[32,32,512]{2,1,0:T(8,128)(2,1)}, bf16[32,32,512]{2,1,0:T(8,128)(2,1)}) fusion(bf16[32,32,1024]{2,1,0:T(8,128)(2,1)S(1)} %all-to-all-done), kind=kLoop, calls=%fused_computation.94 | loop fusion | bytes 4194304 | tf_op jit(solution)/shard_map/slice | solution.py:173
  68.8 1.4 %reshape.325 = bf16[1024,4,128]{2,1,0:T(4,128)(2,1)S(1)} reshape(bf16[32,32,512]{2,1,0:T(8,128)(2,1)} %get-tuple-element.8) | data formatting | bytes 2097152 | tf_op jit(solution)/shard_map/reshape | solution.py:71
  70.2 0.4 fusion.5
  70.6 0.2 concatenate.17
  70.8 1.5 %fusion.50 = (f32[2,8,4]{1,0,2:T(2,128)S(1)}, f32[2,8,4,1090]{3,1,0,2:T(8,128)S(1)}) fusion(f32[2,8,4,1090]{3,1,0,2:T(8,128)S(1)} %concatenate.17), kind=kOutput, calls=%fused_computation.95 | output fusion | flops 210369 | bytes 558336 | tf_op jit(solution)/shard_map/sub | solution.py:96
  72.3 0.1 divide_convert_fusion
  72.4 0.1 slice.44
  72.5 0.3 reshape.327
  72.8 0.3 convolution_bitcast_fusion.1
  73.1 0.0 copy-done
  73.1 0.3 fusion.7
  73.3 0.2 fusion.9
  73.5 0.6 copy.119
  (24 shorter events, 0.2 us)
Async XLA Ops:
  0.0 73.1 %copy-start = (bf16[8,64,512]{2,1,0:T(8,128)(2,1)S(1)}, bf16[8,64,512]{2,1,0:T(8,128)(2,1)}, u32[]{:S(2)}) copy-start(bf16[8,64,512]{2,1,0:T(8,128)(2,1)} %param.24) | copy-start | bytes 1572868
  1.1 9.1 %copy-start.5 = (f32[4096]{0:T(1024)S(1)}, f32[4096]{0:T(1024)}, u32[]{:S(2)}) copy-start(f32[4096]{0:T(1024)} %param.18) | copy-start | bytes 49156
  10.2 3.5 %copy-start.1 = (bf16[512,4096]{1,0:T(8,128)(2,1)S(1)}, bf16[512,4096]{1,0:T(8,128)(2,1)}, u32[]{:S(2)}) copy-start(bf16[512,4096]{1,0:T(8,128)(2,1)} %copy.74) | copy-start | bytes 12582916
  16.4 3.1 %copy-start.2 = (bf16[4096,512]{1,0:T(8,128)(2,1)S(1)}, bf16[4096,512]{1,0:T(8,128)(2,1)}, u32[]{:S(2)}) copy-start(bf16[4096,512]{1,0:T(8,128)(2,1)} %param.20) | copy-start | bytes 12582916
  22.3 10.2 %copy-start.6 = (s32[32,12]{0,1:T(8,128)S(1)}, s32[32,12]{0,1:T(8,128)}, u32[]{:S(2)}) copy-start(s32[32,12]{0,1:T(8,128)} %param.14) | copy-start | bytes 4612
  22.3 10.2 %copy-start.8 = (s32[32,12]{0,1:T(8,128)S(1)}, s32[32,12]{0,1:T(8,128)}, u32[]{:S(2)}) copy-start(s32[32,12]{0,1:T(8,128)} %param.17) | copy-start | bytes 4612
  22.3 10.2 %copy-start.9 = (s32[32,12]{0,1:T(8,128)S(1)}, s32[32,12]{0,1:T(8,128)}, u32[]{:S(2)}) copy-start(s32[32,12]{0,1:T(8,128)} %param.15) | copy-start | bytes 4612
  22.3 10.4 %copy-start.7 = (bf16[2,1,4096]{2,0,1:T(2,128)(2,1)S(1)}, bf16[2,1,4096]{2,0,1:T(2,128)(2,1)}, u32[]{:S(2)}) copy-start(bf16[2,1,4096]{2,0,1:T(2,128)(2,1)} %param.21) | copy-start | bytes 49156
  22.3 39.0 %copy-start.12 = (s32[8]{0:T(128)S(1)}, s32[8]{0:T(128)}, u32[]{:S(2)}) copy-start(s32[8]{0:T(128)} %param.25) | copy-start | bytes 100
  22.3 39.1 %copy-start.10 = (bf16[8,64,512]{2,1,0:T(8,128)(2,1)S(1)}, bf16[8,64,512]{2,1,0:T(8,128)(2,1)}, u32[]{:S(2)}) copy-start(bf16[8,64,512]{2,1,0:T(8,128)(2,1)} %param.23) | copy-start | bytes 1572868
  22.4 39.1 %copy-start.11 = (bf16[2,8,512]{2,1,0:T(8,128)(2,1)S(1)}, bf16[2,8,512]{2,1,0:T(8,128)(2,1)}, u32[]{:S(2)}) copy-start(bf16[2,8,512]{2,1,0:T(8,128)(2,1)} %param.22) | copy-start | bytes 49156
  24.8 42.3 %all-to-all-start = ((bf16[32,32,1024]{2,1,0:T(8,128)(2,1)}), bf16[32,32,1024]{2,1,0:T(8,128)(2,1)S(1)}, u32[]{:S(2)}, u32[]{:S(2)}) async-start(bf16[32,32,1024]{2,1,0:T(8,128)(2,1)} %copy.58), calls=%async_computation | async-start | bytes 4194304 | tf_op jit(solution)/shard_map/all_to_all | solution.py:172
  62.4 4.0 %copy-start.3 = (bf16[4096,512]{1,0:T(8,128)(2,1)S(1)}, bf16[4096,512]{1,0:T(8,128)(2,1)}, u32[]{:S(2)}) copy-start(bf16[4096,512]{1,0:T(8,128)(2,1)} %param.20) | copy-start | bytes 12582916
  68.8 3.7 %copy-start.4 = (bf16[32,32,512]{2,1,0:T(8,128)(2,1)S(1)}, bf16[32,32,512]{2,1,0:T(8,128)(2,1)}, u32[]{:S(2)}) copy-start(bf16[32,32,512]{2,1,0:T(8,128)(2,1)} %get-tuple-element.9) | copy-start | bytes 3145732
where the time goes:
time: 74.5 us; the launch traced here: 74.1 us
  blocking collectives  28.4 us (38%)
  local copies, waits for them, and re-layouts  14.3 us (19%)
  other arithmetic  12.6 us (17%)
  matrix products  10.8 us (14%)
  starting transfers between devices  7.62 us (10%)
    all_gather x1, blocking collectives, per_device(): fresh_all = lax.all_gather(fresh_states, 'tp', axis=1, tiled=True)  28.4 us
    all_to_all x1, starting transfers between devices, per_device(): lax.all_to_all(outbox, 'engine', split_axis=0, concat_axis=0, tiled=True)  7.62 us
    dot_general x1, local copies, waits for them, and re-layouts, project(): key_raw = jnp.dot(normed, key_weight, preferred_element_type=jnp.float32)  6.43 us
    convert_element_type x2, other arithmetic, normalize(): return (widened * factor * norm_gain).astype(jnp.bfloat16)  6.08 us
    dot_general x2, matrix products, project(): key_raw = jnp.dot(normed, key_weight, preferred_element_type=jnp.float32)  5.87 us
    reduce_sum x2, other arithmetic, normalize(): jnp.mean(widened * widened, axis=-1, keepdims=True) + norm_eps  2.81 us
    dot_general x2, matrix products, project(): jnp.dot(normed, value_weight, preferred_element_type=jnp.float32)  2.49 us
    convert_element_type x1, local copies, waits for them, and re-layouts, per_device(): jnp.einsum('ek,kcf->ecf', routing, packed, preferred_element_type=jnp.flo...  2.48 us
  transfers between devices with their start and end apart: 1, of which 0 were waited for; matrix products, arithmetic and copies ran while one was open for 8% of the time, Pallas kernels for 0%

commit v1 on v0

v1 whole, which is shorter than its diff:
```python
import functools
import math

import jax
import jax.numpy as jnp
import numpy as np
from jax import lax
from jax.experimental import pallas as pl
from jax.experimental.pallas import tpu as pltpu
from jax.sharding import PartitionSpec as P

MESH = pl.DeviceIdType.MESH
F32 = jnp.float32
BF16 = jnp.bfloat16
HD = 128
HALF = HD // 2
CTX = 2048
SPAN = 32
ROPE_BASE = 1000000.0
NORM_EPS = 1e-06
NEG = -1e30


def iota(shape, axis):
    return lax.broadcasted_iota(jnp.int32, shape, axis)


def rope_tables(steps):
    frequency = ROPE_BASE ** (-2.0 * np.arange(HALF) / HD)
    blocks = np.arange(CTX // SPAN + 8)[:, None] * SPAN * frequency[None, :]
    tokens = np.arange(SPAN)[:, None] * frequency[None, :]

    def wide(angles):
        cosine, sine = np.cos(angles), np.sin(angles)
        return np.concatenate([cosine, cosine], 1), np.concatenate([-sine, sine], 1)

    return np.concatenate([*wide(blocks), *wide(tokens)], 0).astype(np.float32)


def dot(a, b):
    return jnp.dot(a, b, preferred_element_type=F32)


def dot_nt(a, b):
    return lax.dot_general(a, b, (((1,), (1,)), ((), ())), preferred_element_type=F32)


def per_head(x, count):
    return [x[:, h * HD : (h + 1) * HD] for h in range(count)]


def own_head(x, heads, head_of_row):
    blocks = per_head(x, heads)
    out = blocks[0]
    for h in range(1, heads):
        out = jnp.where(head_of_row == h, blocks[h], out)
    return out


def spread_heads(x, heads, head_of_row):
    return jnp.concatenate(
        [jnp.where(head_of_row == h, x, 0.0) for h in range(heads)], axis=1
    )


def kernel(
    engines,
    tps,
    sends,
    rows,
    steps,
    x_hbm,
    tgt_s,
    blk_s,
    tok_s,
    len_s,
    tgt_v,
    row_v,
    gain_v,
    tab_v,
    fresh_v,
    q_v,
    wk_hbm,
    wv_hbm,
    rk_hbm,
    rv_hbm,
    out_v,
    xv,
    nv,
    wk,
    wv,
    rk,
    rv,
    kb,
    vb,
    cosv,
    sinv,
    fst32,
    fst,
    fin,
    qob,
    qib,
    pob,
    pib,
    sem_x,
    sem_w,
    sem_r,
    sem_f,
    sem_q,
    sem_p,
):
    me = lax.axis_index("engine")
    z = lax.axis_index("tp")
    width = wk.shape[1]
    depth = wk.shape[0]
    heads = width // HD
    sh = steps * heads
    pairs = engines * sh
    inner = sh * rows
    tokens = sends * SPAN
    x_parts = sem_x.shape[0]
    x_rows = tokens // x_parts
    w_parts = sem_w.shape[1]
    w_cols = width // w_parts

    def x_copy(i):
        part = pl.ds(i * x_rows, x_rows)
        return pltpu.make_async_copy(x_hbm.at[part], xv.at[part], sem_x.at[i])

    def w_copy(m, i):
        part = pl.ds(i * w_cols, w_cols)
        source, target = ((wk_hbm, wk), (wv_hbm, wv))[m]
        return pltpu.make_async_copy(source.at[:, part], target.at[:, part], sem_w.at[m, i])

    for i in range(x_parts):
        x_copy(i).start()
    for m in range(2):
        for i in range(w_parts):
            w_copy(m, i).start()
    rk_copy = pltpu.make_async_copy(rk_hbm, rk, sem_r.at[0])
    rv_copy = pltpu.make_async_copy(rv_hbm, rv, sem_r.at[1])
    rk_copy.start()
    rv_copy.start()

    barrier = pltpu.get_barrier_semaphore()

    def greet_engine(i, carry):
        other = lax.rem(me + i, engines)
        pl.semaphore_signal(barrier, inc=1, device_id=(other, z), device_id_type=MESH)
        return carry

    def greet_tp(i, carry):
        other = lax.rem(z + i, tps)
        pl.semaphore_signal(barrier, inc=1, device_id=(me, other), device_id_type=MESH)
        return carry

    lax.fori_loop(1, engines, greet_engine, 0)
    lax.fori_loop(1, tps, greet_tp, 0)

    gain = gain_v[...]
    fw = depth // 8
    fresh = fresh_v[...].astype(F32)
    fresh = fresh * lax.rsqrt(jnp.mean(fresh * fresh, axis=1, keepdims=True) + NORM_EPS) * gain
    for s in range(steps):
        for c in range(8):
            fst32[s * 8 + c : s * 8 + c + 1, :] = fresh[s : s + 1, c * fw : (c + 1) * fw]
    fst[...] = fst32[...].astype(BF16)
    fin[z] = fst[...]

    q = q_v[...].astype(F32)
    q64 = jnp.concatenate(
        [q[s][:, h * HD : (h + 1) * HD] for s in range(steps) for h in range(heads)], axis=0
    )
    hit = tgt_v[...] == me
    arrives = jnp.sum(jnp.where(hit, (row_v[...] + 1).astype(F32), 0.0), axis=0, keepdims=True)
    pe = iota((pairs, engines), 0) // sh
    row_col = jnp.sum(
        jnp.where(pe == iota((pairs, engines), 1), arrives, 0.0), axis=1, keepdims=True
    )
    arr_col = jnp.sum(
        jnp.where(
            iota((engines, engines), 0) == iota((engines, engines), 1), arrives, 0.0
        ),
        axis=1,
        keepdims=True,
    )
    row_lane = jnp.sum(
        jnp.where(
            iota((engines, pairs), 0) == iota((engines, pairs), 1) // sh, arr_col, 0.0
        ),
        axis=0,
        keepdims=True,
    )
    gi, gl = iota((pairs, inner), 0), iota((pairs, inner), 1)
    pick = (row_col == (gl % rows + 1).astype(F32)) & (gi % sh == gl // rows)
    ti, tl = iota((inner, pairs), 0), iota((inner, pairs), 1)
    pick_t = (row_lane == (ti % rows + 1).astype(F32)) & (tl % sh == ti // rows)
    qout = dot(jnp.where(pick, 1.0, 0.0).astype(BF16), q64.astype(BF16))
    qob[...] = qout.reshape(engines, sh, HD)
    qib[me] = jnp.zeros((sh, HD), F32)

    pl.semaphore_wait(barrier, engines - 1 + tps - 1)

    def q_copy(i):
        other = lax.rem(me + i, engines)
        return pltpu.make_async_remote_copy(
            src_ref=qob.at[other],
            dst_ref=qib.at[me],
            send_sem=sem_q.at[0],
            recv_sem=sem_q.at[1],
            device_id=(other, z),
            device_id_type=MESH,
        )

    def f_copy(i):
        other = lax.rem(z + i, tps)
        return pltpu.make_async_remote_copy(
            src_ref=fst,
            dst_ref=fin.at[z],
            send_sem=sem_f.at[0],
            recv_sem=sem_f.at[1],
            device_id=(me, other),
            device_id_type=MESH,
        )

    def start_q(i, carry):
        q_copy(i).start()
        return carry

    def start_f(i, carry):
        f_copy(i).start()
        return carry

    lax.fori_loop(1, engines, start_q, 0)
    lax.fori_loop(1, tps, start_f, 0)

    nb = CTX // SPAN + 8
    tok_cos = tab_v[2 * nb : 2 * nb + SPAN, :]
    tok_sin = tab_v[2 * nb + SPAN : 2 * nb + 2 * SPAN, :]
    lane_token = iota((1, tokens), 1)
    col_target = jnp.full((1, tokens), -1, jnp.int32)
    for k in range(sends):
        b = blk_s[k, me]
        block_cos = tab_v[pl.ds(b, 1), :]
        block_sin = tab_v[pl.ds(b + nb, 1), :]
        cosv[k * SPAN : (k + 1) * SPAN, :] = block_cos * tok_cos - block_sin * tok_sin
        sinv[k * SPAN : (k + 1) * SPAN, :] = block_sin * tok_cos + block_cos * tok_sin
        live = (lane_token >= k * SPAN) & (lane_token < k * SPAN + tok_s[k, me])
        col_target = jnp.where(live, tgt_s[k, me], col_target)

    for i in range(x_parts):
        x_copy(i).wait()

        def norm_step(j, carry, i=i):
            part = pl.ds(pl.multiple_of(i * x_rows + j * 16, 16), 16)
            block = xv[part, :].astype(F32)
            factor = lax.rsqrt(jnp.mean(block * block, axis=1, keepdims=True) + NORM_EPS)
            nv[part, :] = (block * factor * gain).astype(BF16)
            return carry

        lax.fori_loop(0, x_rows // 16, norm_step, 0)

    def turn(raw, cosine, sine):
        return raw * cosine + pltpu.roll(raw, HALF, 1) * sine

    for i in range(w_parts):
        w_copy(0, i).wait()
        raw = dot(nv[...], wk[:, i * w_cols : (i + 1) * w_cols])
        for h in range(w_cols // HD):
            turned = turn(raw[:, h * HD : (h + 1) * HD], cosv[...], sinv[...])
            kb[:, i * w_cols + h * HD : i * w_cols + (h + 1) * HD] = turned.astype(BF16)
    for i in range(w_parts):
        w_copy(1, i).wait()
        vb[:, i * w_cols : (i + 1) * w_cols] = dot(
            nv[...], wv[:, i * w_cols : (i + 1) * w_cols]
        ).astype(BF16)

    scale = 1.0 / math.sqrt(HD)
    everyone = pltpu.make_async_remote_copy(
        src_ref=qob.at[pl.ds(0, engines - 1)],
        dst_ref=qib.at[pl.ds(0, engines - 1)],
        send_sem=sem_q.at[0],
        recv_sem=sem_q.at[1],
        device_id=(me, z),
        device_id_type=MESH,
    )
    everyone.wait_recv()
    pair_row = iota((pairs, 1), 0)
    pair_head = pair_row % heads
    qin = qib[...].reshape(pairs, HD)
    s = dot_nt(spread_heads(qin, heads, pair_head).astype(BF16), kb[...]) * scale
    live = col_target == pair_row // sh
    s = jnp.where(live, s, NEG)
    peak = jnp.max(s, axis=1, keepdims=True)
    p = jnp.where(live, jnp.exp(s - peak), 0.0)
    total = jnp.maximum(jnp.sum(p, axis=1, keepdims=True), 1e-30)
    o = own_head(dot(p.astype(BF16), vb[...]), heads, pair_head) / total
    lse = peak + jnp.log(total)
    hi = lse.astype(BF16).astype(F32)
    mid = (lse - hi).astype(BF16).astype(F32)
    low = lse - hi - mid
    lane = iota((pairs, HD), 1)
    coded = jnp.where(lane < 32, hi, jnp.where(lane < 64, mid, low))
    pob[...] = jnp.concatenate(
        [o.reshape(engines, sh, HD), coded.reshape(engines, sh, HD)], axis=1
    ).astype(BF16)

    def p_copy(i):
        other = lax.rem(me + i, engines)
        return pltpu.make_async_remote_copy(
            src_ref=pob.at[other],
            dst_ref=pib.at[me],
            send_sem=sem_p.at[0],
            recv_sem=sem_p.at[1],
            device_id=(other, z),
            device_id_type=MESH,
        )

    def start_p(i, carry):
        p_copy(i).start()
        return carry

    lax.fori_loop(1, engines, start_p, 0)
    pib[me] = jnp.zeros((2 * sh, HD), BF16)

    fresh_all = pltpu.make_async_remote_copy(
        src_ref=fin.at[pl.ds(0, tps - 1)],
        dst_ref=fin.at[pl.ds(0, tps - 1)],
        send_sem=sem_f.at[0],
        recv_sem=sem_f.at[1],
        device_id=(me, z),
        device_id_type=MESH,
    )
    fresh_all.wait_recv()
    fr = rows * steps * 8
    ri, rl = iota((fr, fr), 0), iota((fr, fr), 1)
    want = (ri % rows) * (steps * 8) + (ri // rows % steps) * 8 + ri // (rows * steps)
    order = jnp.where(rl == want, 1.0, 0.0).astype(BF16)
    sorted_fresh = dot(order, fin[...].reshape(fr, fw)).astype(BF16)
    new = rows * steps
    fn = jnp.concatenate(
        [sorted_fresh[c * new : (c + 1) * new, :] for c in range(8)], axis=1
    )
    f_step = iota((new, 1), 0) // rows
    f_cos = jnp.zeros((new, HD), F32)
    f_sin = jnp.zeros((new, HD), F32)
    bc = CTX // SPAN
    for t in range(steps):
        c0, s0 = tab_v[bc : bc + 1, :], tab_v[nb + bc : nb + bc + 1, :]
        c1, s1 = tok_cos[t : t + 1, :], tok_sin[t : t + 1, :]
        f_cos = jnp.where(f_step == t, c0 * c1 - s0 * s1, f_cos)
        f_sin = jnp.where(f_step == t, s0 * c1 + c0 * s1, f_sin)
    raw = dot(fn, wk[...])
    fk = jnp.concatenate([turn(b, f_cos, f_sin) for b in per_head(raw, heads)], axis=1).astype(BF16)
    fv = dot(fn, wv[...]).astype(BF16)

    near = rk.shape[0]
    resident = near // rows
    rk_copy.wait()
    rv_copy.wait()
    in_row = iota((inner, 1), 0)
    in_head = in_row // rows % heads
    q_near = spread_heads(q64, heads, in_head).astype(BF16)
    lane_near = iota((1, near), 1)
    col_row = jnp.full((1, near), -1, jnp.int32)
    for r in range(rows):
        ok = (lane_near >= r * resident) & (lane_near < r * resident + len_s[r])
        col_row = jnp.where(ok, r, col_row)
    live_near = col_row == in_row % rows
    lane_new = iota((1, new), 1)
    live_new = (lane_new % rows == in_row % rows) & (lane_new // rows <= in_row // (rows * heads))
    s_near = jnp.where(live_near, dot_nt(q_near, rk[...]) * scale, NEG)
    s_new = jnp.where(live_new, dot_nt(q_near, fk) * scale, NEG)
    peak_n = jnp.maximum(
        jnp.max(s_near, axis=1, keepdims=True), jnp.max(s_new, axis=1, keepdims=True)
    )
    p_near = jnp.where(live_near, jnp.exp(s_near - peak_n), 0.0)
    p_new = jnp.where(live_new, jnp.exp(s_new - peak_n), 0.0)
    total_n = jnp.sum(p_near, axis=1, keepdims=True) + jnp.sum(p_new, axis=1, keepdims=True)
    o_near = own_head(
        dot(p_near.astype(BF16), rv[...]) + dot(p_new.astype(BF16), fv), heads, in_head
    )

    from_all = pltpu.make_async_remote_copy(
        src_ref=pob.at[pl.ds(0, engines - 1)],
        dst_ref=pib.at[pl.ds(0, engines - 1)],
        send_sem=sem_p.at[0],
        recv_sem=sem_p.at[1],
        device_id=(me, z),
        device_id_type=MESH,
    )
    from_all.wait_recv()
    pin = pib[...].astype(F32)
    o_in = pin[:, :sh, :].reshape(pairs, HD)
    parts = pin[:, sh:, :].reshape(pairs, HD)
    lse_in = parts[:, 0:1] + parts[:, 32:33] + parts[:, 64:65]
    eye = iota((inner, inner), 0) == iota((inner, inner), 1)
    peak_lane = jnp.sum(jnp.where(eye, peak_n, 0.0), axis=0, keepdims=True)
    top = jnp.maximum(
        jnp.max(jnp.where(pick, lse_in, NEG), axis=0, keepdims=True), peak_lane
    )
    top_pair = jnp.sum(jnp.where(pick, top, 0.0), axis=1, keepdims=True)
    top_in = jnp.sum(jnp.where(eye, top, 0.0), axis=1, keepdims=True)
    valid = row_col > 0.0
    w_in = jnp.where(valid, jnp.exp(jnp.where(valid, lse_in - top_pair, 0.0)), 0.0)
    weighted = jnp.concatenate(
        [jnp.where(valid, w_in * o_in, 0.0), jnp.broadcast_to(w_in, (pairs, HD))], axis=1
    )
    first = weighted.astype(BF16)
    second = (weighted - first.astype(F32)).astype(BF16)
    collect = jnp.where(pick_t, 1.0, 0.0).astype(BF16)
    gathered = dot(collect, first) + dot(collect, second)
    w_near = jnp.exp(peak_n - top_in)
    result = (w_near * o_near + gathered[:, :HD]) / (w_near * total_n + gathered[:, HD:])
    for t in range(steps):
        for h in range(heads):
            j = t * heads + h
            out_v[t, :, h * HD : (h + 1) * HD] = result[j * rows : (j + 1) * rows, :].astype(BF16)

    everyone.wait_send()
    fresh_all.wait_send()
    from_all.wait_send()


def per_device(
    engines,
    tps,
    outgoing,
    span_target,
    span_row,
    span_block,
    span_tokens,
    norm_gain,
    key_weight,
    value_weight,
    fresh_states,
    queries,
    res_keys,
    res_values,
    res_len,
):
    sends, span, depth = outgoing.shape
    width = key_weight.shape[1]
    steps, rows, _ = queries.shape
    resident = res_keys.shape[1]
    heads = width // HD
    sh = steps * heads
    tokens = sends * span
    vmem = pl.BlockSpec(memory_space=pltpu.VMEM)
    smem = pl.BlockSpec(memory_space=pltpu.SMEM)
    hbm = pl.BlockSpec(memory_space=pltpu.HBM)
    target_t = span_target.T
    x_parts, w_parts = 3, 2
    return pl.pallas_call(
        functools.partial(kernel, engines, tps, sends, rows, steps),
        out_shape=jax.ShapeDtypeStruct((steps, rows, width), BF16),
        in_specs=[hbm, smem, smem, smem, smem, vmem, vmem, vmem, vmem, vmem, vmem, hbm, hbm, hbm, hbm],
        out_specs=vmem,
        scratch_shapes=[
            pltpu.VMEM((tokens, depth), BF16),
            pltpu.VMEM((tokens, depth), BF16),
            pltpu.VMEM((depth, width), BF16),
            pltpu.VMEM((depth, width), BF16),
            pltpu.VMEM((rows * resident, width), BF16),
            pltpu.VMEM((rows * resident, width), BF16),
            pltpu.VMEM((tokens, width), BF16),
            pltpu.VMEM((tokens, width), BF16),
            pltpu.VMEM((tokens, HD), F32),
            pltpu.VMEM((tokens, HD), F32),
            pltpu.VMEM((steps * 8, depth // 8), F32),
            pltpu.VMEM((steps * 8, depth // 8), BF16),
            pltpu.VMEM((tps, steps * 8, depth // 8), BF16),
            pltpu.VMEM((engines, sh, HD), F32),
            pltpu.VMEM((engines, sh, HD), F32),
            pltpu.VMEM((engines, 2 * sh, HD), BF16),
            pltpu.VMEM((engines, 2 * sh, HD), BF16),
            pltpu.SemaphoreType.DMA((x_parts,)),
            pltpu.SemaphoreType.DMA((2, w_parts)),
            pltpu.SemaphoreType.DMA((2,)),
            pltpu.SemaphoreType.DMA((2,)),
            pltpu.SemaphoreType.DMA((2,)),
            pltpu.SemaphoreType.DMA((2,)),
        ],
        compiler_params=pltpu.CompilerParams(
            collective_id=0, has_side_effects=True, vmem_limit_bytes=60 * 1024 * 1024
        ),
    )(
        outgoing.reshape(tokens, depth),
        target_t,
        span_block.T,
        span_tokens.T,
        res_len,
        target_t,
        span_row.T,
        norm_gain.reshape(1, depth),
        jnp.asarray(rope_tables(steps)),
        fresh_states.reshape(steps, depth),
        queries,
        key_weight,
        value_weight,
        res_keys.reshape(rows * resident, width),
        res_values.reshape(rows * resident, width),
    )


def solution(mesh):
    in_specs = (
        P("engine", None, None),
        P(),
        P(),
        P(),
        P(),
        P(),
        P(None, "tp"),
        P(None, "tp"),
        P(None, ("engine", "tp"), None),
        P(None, "engine", "tp"),
        P("engine", None, "tp"),
        P("engine", None, "tp"),
        P("engine"),
    )
    return jax.shard_map(
        functools.partial(per_device, mesh.shape["engine"], mesh.shape["tp"]),
        mesh=mesh,
        in_specs=in_specs,
        out_specs=P(None, "engine", "tp"),
        check_vma=False,
    )
```

time: 74.5 us -> 32.2 us (0.43)
  the two profiles are of different devices: /device:TPU:2 before, /device:TPU:1 now
where the time goes in v1:
time: 32.2 us; the launch traced here: 32 us
  Pallas kernels  30.7 us (95%)
  local copies, waits for them, and re-layouts  1.32 us (4%)
    pallas_call x1, Pallas kernels, per_device(): pl.pallas_call(functools.partial(kernel, engines, tps, sends, rows, steps...  30.7 us
    unnamed x1, local copies, waits for them, and re-layouts  1.32 us

profile of v1, /device:TPU:1, one launch (start us, length us, event | category | flops | bytes accessed | tf_op | source)
XLA Modules:
  0.0 32.0 jit_solution(13492587174080776877)
XLA Ops:
  0.0 30.7 %shard_map.136 = bf16[2,8,512]{2,1,0:T(8,128)(2,1)} custom-call(bf16[384,4096]{1,0:T(8,128)(2,1)} %bitcast.9, s32[12,32]{1,0:T(8,128)} %bitcast.12, s32[12,32]{1,0:T(8,128)} %bitcast.16, s32[12,32]{1,0:T(8,128)} %bitcast.17, s32[8]{0:T(128)} %len_s.1, s32[12,32]{1,0:T(8,128)} %bitcast.13, s32[12,32]{1,0:T(8,128)} %bitcast.18, f32[1,4096]{1,0:T(1,128)} %bitcast.14, ...), custom_call_target="tpu_custom_call" | custom-call | tf_op jit(solution)/shard_map/pallas_call | solution.py:454
  30.7 1.3 %copy.16 = bf16[2,8,512]{2,1,0:T(8,128)(2,1)} copy(bf16[2,8,512]{2,1,0:T(8,128)(2,1)} %shard_map.136) | data formatting | bytes 32768

commit v2 on v1

--- a/solution.py
+++ b/solution.py
@@ -70,16 +70,15 @@
     rows,
     steps,
     x_hbm,
-    tgt_s,
-    blk_s,
-    tok_s,
-    len_s,
-    tgt_v,
-    row_v,
-    gain_v,
-    tab_v,
-    fresh_v,
-    q_v,
+    tgt_hbm,
+    row_hbm,
+    blk_hbm,
+    tok_hbm,
+    len_hbm,
+    gain_hbm,
+    tab_hbm,
+    fresh_hbm,
+    q_hbm,
     wk_hbm,
     wv_hbm,
     rk_hbm,
@@ -91,8 +90,11 @@
     wv,
     rk,
     rv,
+    ak,
+    av,
     kb,
     vb,
+    squares,
     cosv,
     sinv,
     fst32,
@@ -102,9 +104,21 @@
     qib,
     pob,
     pib,
+    place,
+    tgt_s,
+    blk_s,
+    tok_s,
+    len_s,
+    tgt_v,
+    row_v,
+    gain_v,
+    tab_v,
+    fresh_v,
+    q_v,
     sem_x,
     sem_w,
     sem_r,
+    sem_s,
     sem_f,
     sem_q,
     sem_p,
@@ -118,25 +132,46 @@
     pairs = engines * sh
     inner = sh * rows
     tokens = sends * SPAN
-    x_parts = sem_x.shape[0]
-    x_rows = tokens // x_parts
-    w_parts = sem_w.shape[1]
-    w_cols = width // w_parts
-
-    def x_copy(i):
-        part = pl.ds(i * x_rows, x_rows)
-        return pltpu.make_async_copy(x_hbm.at[part], xv.at[part], sem_x.at[i])
-
-    def w_copy(m, i):
-        part = pl.ds(i * w_cols, w_cols)
+    chunks = sem_x.shape[0]
+    chunk = depth // chunks
+
+    def x_copy(c):
+        part = pl.ds(c * chunk, chunk)
+        return pltpu.make_async_copy(x_hbm.at[:, part], xv.at[:, part], sem_x.at[c])
+
+    def w_copy(m, c):
+        part = pl.ds(c * chunk, chunk)
         source, target = ((wk_hbm, wk), (wv_hbm, wv))[m]
-        return pltpu.make_async_copy(source.at[:, part], target.at[:, part], sem_w.at[m, i])
-
-    for i in range(x_parts):
-        x_copy(i).start()
-    for m in range(2):
-        for i in range(w_parts):
-            w_copy(m, i).start()
+        return pltpu.make_async_copy(source.at[part], target.at[part], sem_w.at[m, c])
+
+    small = [
+        pltpu.make_async_copy(source, target, sem_s.at[i])
+        for i, (source, target) in enumerate(
+            (
+                (gain_hbm, gain_v),
+                (fresh_hbm, fresh_v),
+                (q_hbm, q_v),
+                (tgt_hbm, tgt_v),
+                (row_hbm, row_v),
+                (tgt_hbm, tgt_s),
+                (blk_hbm, blk_s),
+                (tok_hbm, tok_s),
+                (tab_hbm, tab_v),
+                (len_hbm, len_s),
+            )
+        )
+    ]
+    x_copy(0).start()
+    for copy in small[:5]:
+        copy.start()
+    for c in range(chunks):
+        w_copy(0, c).start()
+        w_copy(1, c).start()
+        if c + 1 < chunks:
+            x_copy(c + 1).start()
+        if c == 0:
+            for copy in small[5:]:
+                copy.start()
     rk_copy = pltpu.make_async_copy(rk_hbm, rk, sem_r.at[0])
     rv_copy = pltpu.make_async_copy(rv_hbm, rv, sem_r.at[1])
     rk_copy.start()
@@ -157,16 +192,20 @@
     lax.fori_loop(1, engines, greet_engine, 0)
     lax.fori_loop(1, tps, greet_tp, 0)
 
-    gain = gain_v[...]
+    small[0].wait()
+    small[1].wait()
     fw = depth // 8
     fresh = fresh_v[...].astype(F32)
-    fresh = fresh * lax.rsqrt(jnp.mean(fresh * fresh, axis=1, keepdims=True) + NORM_EPS) * gain
+    fresh = fresh * lax.rsqrt(jnp.mean(fresh * fresh, axis=1, keepdims=True) + NORM_EPS)
+    fresh = fresh * gain_v[...]
     for s in range(steps):
         for c in range(8):
             fst32[s * 8 + c : s * 8 + c + 1, :] = fresh[s : s + 1, c * fw : (c + 1) * fw]
     fst[...] = fst32[...].astype(BF16)
     fin[z] = fst[...]
 
+    for copy in small[2:5]:
+        copy.wait()
     q = q_v[...].astype(F32)
     q64 = jnp.concatenate(
         [q[s][:, h * HD : (h + 1) * HD] for s in range(steps) for h in range(heads)], axis=0
@@ -199,7 +238,22 @@
     qob[...] = qout.reshape(engines, sh, HD)
     qib[me] = jnp.zeros((sh, HD), F32)
 
-    pl.semaphore_wait(barrier, engines - 1 + tps - 1)
+    for copy in small[5:]:
+        copy.wait()
+    nb = CTX // SPAN + 8
+    tok_cos = tab_v[2 * nb : 2 * nb + SPAN, :]
+    tok_sin = tab_v[2 * nb + SPAN : 2 * nb + 2 * SPAN, :]
+    span_lane = iota((1, sends * sh), 1)
+    lane_target = jnp.full((1, sends * sh), -1, jnp.int32)
+    for k in range(sends):
+        b = blk_s[k, me]
+        block_cos = tab_v[pl.ds(b, 1), :]
+        block_sin = tab_v[pl.ds(b + nb, 1), :]
+        cosv[k * SPAN : (k + 1) * SPAN, :] = block_cos * tok_cos - block_sin * tok_sin
+        sinv[k * SPAN : (k + 1) * SPAN, :] = block_sin * tok_cos + block_cos * tok_sin
+        lane_target = jnp.where(span_lane // sh == k, tgt_s[k, me], lane_target)
+    oi, ol = iota((pairs, sends * sh), 0), iota((pairs, sends * sh), 1)
+    place[...] = jnp.where((lane_target == oi // sh) & (oi % sh == ol % sh), 1.0, 0.0).astype(BF16)
 
     def q_copy(i):
         other = lax.rem(me + i, engines)
@@ -231,49 +285,43 @@
         f_copy(i).start()
         return carry
 
-    lax.fori_loop(1, engines, start_q, 0)
-    lax.fori_loop(1, tps, start_f, 0)
-
-    nb = CTX // SPAN + 8
-    tok_cos = tab_v[2 * nb : 2 * nb + SPAN, :]
-    tok_sin = tab_v[2 * nb + SPAN : 2 * nb + 2 * SPAN, :]
-    lane_token = iota((1, tokens), 1)
-    col_target = jnp.full((1, tokens), -1, jnp.int32)
-    for k in range(sends):
-        b = blk_s[k, me]
-        block_cos = tab_v[pl.ds(b, 1), :]
-        block_sin = tab_v[pl.ds(b + nb, 1), :]
-        cosv[k * SPAN : (k + 1) * SPAN, :] = block_cos * tok_cos - block_sin * tok_sin
-        sinv[k * SPAN : (k + 1) * SPAN, :] = block_sin * tok_cos + block_cos * tok_sin
-        live = (lane_token >= k * SPAN) & (lane_token < k * SPAN + tok_s[k, me])
-        col_target = jnp.where(live, tgt_s[k, me], col_target)
-
-    for i in range(x_parts):
-        x_copy(i).wait()
-
-        def norm_step(j, carry, i=i):
-            part = pl.ds(pl.multiple_of(i * x_rows + j * 16, 16), 16)
-            block = xv[part, :].astype(F32)
-            factor = lax.rsqrt(jnp.mean(block * block, axis=1, keepdims=True) + NORM_EPS)
-            nv[part, :] = (block * factor * gain).astype(BF16)
-            return carry
-
-        lax.fori_loop(0, x_rows // 16, norm_step, 0)
-
     def turn(raw, cosine, sine):
         return raw * cosine + pltpu.roll(raw, HALF, 1) * sine
 
-    for i in range(w_parts):
-        w_copy(0, i).wait()
-        raw = dot(nv[...], wk[:, i * w_cols : (i + 1) * w_cols])
-        for h in range(w_cols // HD):
-            turned = turn(raw[:, h * HD : (h + 1) * HD], cosv[...], sinv[...])
-            kb[:, i * w_cols + h * HD : i * w_cols + (h + 1) * HD] = turned.astype(BF16)
-    for i in range(w_parts):
-        w_copy(1, i).wait()
-        vb[:, i * w_cols : (i + 1) * w_cols] = dot(
-            nv[...], wv[:, i * w_cols : (i + 1) * w_cols]
-        ).astype(BF16)
+    for c in range(chunks):
+        part = slice(c * chunk, (c + 1) * chunk)
+        x_copy(c).wait()
+        block = xv[:, part].astype(F32)
+        nv[:, part] = (block * gain_v[:, part]).astype(BF16)
+        sq = block * block
+        folded = sum(sq[:, j * HD : (j + 1) * HD] for j in range(chunk // HD))
+        squares[...] = folded if c == 0 else squares[...] + folded
+        last = c == chunks - 1
+        if last:
+            mean = jnp.sum(squares[...], axis=1, keepdims=True) * (1.0 / depth)
+            factor = lax.rsqrt(mean + NORM_EPS)
+            cosv[...] = cosv[...] * factor
+            sinv[...] = sinv[...] * factor
+        w_copy(0, c).wait()
+        raw = dot(nv[:, part], wk[part, :])
+        raw = raw if c == 0 else ak[...] + raw
+        if last:
+            for h in range(heads):
+                head = slice(h * HD, (h + 1) * HD)
+                kb[:, head] = turn(raw[:, head], cosv[...], sinv[...]).astype(BF16)
+        else:
+            ak[...] = raw
+        w_copy(1, c).wait()
+        raw = dot(nv[:, part], wv[part, :])
+        raw = raw if c == 0 else av[...] + raw
+        if last:
+            vb[...] = (raw * factor).astype(BF16)
+        else:
+            av[...] = raw
+        if c == chunks // 2 - 1:
+            pl.semaphore_wait(barrier, engines - 1 + tps - 1)
+            lax.fori_loop(1, engines, start_q, 0)
+            lax.fori_loop(1, tps, start_f, 0)
 
     scale = 1.0 / math.sqrt(HD)
     everyone = pltpu.make_async_remote_copy(
@@ -285,24 +333,34 @@
         device_id_type=MESH,
     )
     everyone.wait_recv()
-    pair_row = iota((pairs, 1), 0)
-    pair_head = pair_row % heads
-    qin = qib[...].reshape(pairs, HD)
-    s = dot_nt(spread_heads(qin, heads, pair_head).astype(BF16), kb[...]) * scale
-    live = col_target == pair_row // sh
-    s = jnp.where(live, s, NEG)
-    peak = jnp.max(s, axis=1, keepdims=True)
-    p = jnp.where(live, jnp.exp(s - peak), 0.0)
-    total = jnp.maximum(jnp.sum(p, axis=1, keepdims=True), 1e-30)
-    o = own_head(dot(p.astype(BF16), vb[...]), heads, pair_head) / total
-    lse = peak + jnp.log(total)
-    hi = lse.astype(BF16).astype(F32)
-    mid = (lse - hi).astype(BF16).astype(F32)
-    low = lse - hi - mid
-    lane = iota((pairs, HD), 1)
-    coded = jnp.where(lane < 32, hi, jnp.where(lane < 64, mid, low))
+    made = []
+    for g in range(0, sends, HD // SPAN):
+        spans = range(g, min(g + HD // SPAN, sends))
+        count = len(spans)
+        group = slice(g * SPAN, (g + count) * SPAN)
+        q_g = jnp.concatenate([qib[tgt_s[k, me]] for k in spans], axis=0)
+        g_row = iota((count * sh, 1), 0)
+        g_lane = iota((1, count * SPAN), 1)
+        edge = jnp.zeros((count * sh, 1), jnp.int32)
+        for j, k in enumerate(spans):
+            edge = jnp.where(g_row // sh == j, j * SPAN + tok_s[k, me], edge)
+        live = (g_lane >= g_row // sh * SPAN) & (g_lane < edge)
+        s = dot_nt(spread_heads(q_g, heads, g_row % heads).astype(BF16), kb[group, :]) * scale
+        s = jnp.where(live, s, NEG)
+        peak = jnp.max(s, axis=1, keepdims=True)
+        p = jnp.where(live, jnp.exp(s - peak), 0.0)
+        total = jnp.sum(p, axis=1, keepdims=True)
+        o = own_head(dot(p.astype(BF16), vb[group, :]), heads, g_row % heads) / total
+        lse = peak + jnp.log(total)
+        hi = lse.astype(BF16).astype(F32)
+        mid = (lse - hi).astype(BF16).astype(F32)
+        low = lse - hi - mid
+        lane = iota((count * sh, HD), 1)
+        coded = jnp.where(lane < 32, hi, jnp.where(lane < 64, mid, low))
+        made.append(jnp.concatenate([o, coded], axis=1).astype(BF16))
+    placed = dot(place[...], jnp.concatenate(made, axis=0))
     pob[...] = jnp.concatenate(
-        [o.reshape(engines, sh, HD), coded.reshape(engines, sh, HD)], axis=1
+        [placed[:, :HD].reshape(engines, sh, HD), placed[:, HD:].reshape(engines, sh, HD)], axis=1
     ).astype(BF16)
 
     def p_copy(i):
@@ -447,14 +505,13 @@
     sh = steps * heads
     tokens = sends * span
     vmem = pl.BlockSpec(memory_space=pltpu.VMEM)
-    smem = pl.BlockSpec(memory_space=pltpu.SMEM)
     hbm = pl.BlockSpec(memory_space=pltpu.HBM)
-    target_t = span_target.T
-    x_parts, w_parts = 3, 2
+    chunks = 8
+    table = jnp.asarray(rope_tables(steps))
     return pl.pallas_call(
         functools.partial(kernel, engines, tps, sends, rows, steps),
         out_shape=jax.ShapeDtypeStruct((steps, rows, width), BF16),
-        in_specs=[hbm, smem, smem, smem, smem, vmem, vmem, vmem, vmem, vmem, vmem, hbm, hbm, hbm, hbm],
+        in_specs=[hbm] * 14,
         out_specs=vmem,
         scratch_shapes=[
             pltpu.VMEM((tokens, depth), BF16),
@@ -463,8 +520,11 @@
             pltpu.VMEM((depth, width), BF16),
             pltpu.VMEM((rows * resident, width), BF16),
             pltpu.VMEM((rows * resident, width), BF16),
+            pltpu.VMEM((tokens, width), F32),
+            pltpu.VMEM((tokens, width), F32),
             pltpu.VMEM((tokens, width), BF16),
             pltpu.VMEM((tokens, width), BF16),
+            pltpu.VMEM((tokens, HD), F32),
             pltpu.VMEM((tokens, HD), F32),
             pltpu.VMEM((tokens, HD), F32),
             pltpu.VMEM((steps * 8, depth // 8), F32),
@@ -474,9 +534,21 @@
             pltpu.VMEM((engines, sh, HD), F32),
             pltpu.VMEM((engines, 2 * sh, HD), BF16),
             pltpu.VMEM((engines, 2 * sh, HD), BF16),
-            pltpu.SemaphoreType.DMA((x_parts,)),
-            pltpu.SemaphoreType.DMA((2, w_parts)),
+            pltpu.VMEM((engines * sh, sends * sh), BF16),
+            pltpu.SMEM((sends, engines), jnp.int32),
+            pltpu.SMEM((sends, engines), jnp.int32),
+            pltpu.SMEM((sends, engines), jnp.int32),
+            pltpu.SMEM((rows,), jnp.int32),
+            pltpu.VMEM((sends, engines), jnp.int32),
+            pltpu.VMEM((sends, engines), jnp.int32),
+            pltpu.VMEM((1, depth), F32),
+            pltpu.VMEM(table.shape, F32),
+            pltpu.VMEM((steps, depth), BF16),
+            pltpu.VMEM((steps, rows, width), BF16),
+            pltpu.SemaphoreType.DMA((chunks,)),
+            pltpu.SemaphoreType.DMA((2, chunks)),
             pltpu.SemaphoreType.DMA((2,)),
+            pltpu.SemaphoreType.DMA((10,)),
             pltpu.SemaphoreType.DMA((2,)),
             pltpu.SemaphoreType.DMA((2,)),
             pltpu.SemaphoreType.DMA((2,)),
@@ -486,14 +558,13 @@
         ),
     )(
         outgoing.reshape(tokens, depth),
-        target_t,
+        span_target.T,
+        span_row.T,
         span_block.T,
         span_tokens.T,
         res_len,
-        target_t,
-        span_row.T,
         norm_gain.reshape(1, depth),
-        jnp.asarray(rope_tables(steps)),
+        table,
         fresh_states.reshape(steps, depth),
         queries,
         key_weight,

time: 32.2 us -> 24.9 us (0.77)
  Pallas kernels: 30.7 us -> 23.4 us
    pallas_call x1, Pallas kernels: 30.7 us -> 23.4 us  [per_device(): pl.pallas_call(functools.partial(kernel, engines, tps, sends, rows, steps...]
where the time goes in v2:
time: 24.9 us; the launch traced here: 24.7 us
  Pallas kernels  23.4 us (94%)
  local copies, waits for them, and re-layouts  1.32 us (5%)
    pallas_call x1, Pallas kernels, per_device(): pl.pallas_call(functools.partial(kernel, engines, tps, sends, rows, steps...  23.4 us
    unnamed x1, local copies, waits for them, and re-layouts  1.32 us

profile of v2, /device:TPU:1, one launch (start us, length us, event | category | flops | bytes accessed | tf_op | source)
XLA Modules:
  0.0 24.7 jit_solution(3685806635949499591)
XLA Ops:
  0.0 23.4 %shard_map.136 = bf16[2,8,512]{2,1,0:T(8,128)(2,1)} custom-call(bf16[384,4096]{1,0:T(8,128)(2,1)} %bitcast.9, s32[12,32]{1,0:T(8,128)} %bitcast.14, s32[12,32]{1,0:T(8,128)} %bitcast.15, s32[12,32]{1,0:T(8,128)} %bitcast.16, s32[12,32]{1,0:T(8,128)} %bitcast.17, s32[8]{0:T(128)} %len_hbm.1, f32[1,4096]{1,0:T(1,128)} %bitcast.12, ...), custom_call_target="tpu_custom_call" | custom-call | tf_op jit(solution)/shard_map/pallas_call | solution.py:511
  23.4 1.3 %copy.16 = bf16[2,8,512]{2,1,0:T(8,128)(2,1)} copy(bf16[2,8,512]{2,1,0:T(8,128)(2,1)} %shard_map.136) | data formatting | bytes 32768

commit v3 on v2

--- a/solution.py
+++ b/solution.py
@@ -35,6 +35,20 @@
         return np.concatenate([cosine, cosine], 1), np.concatenate([-sine, sine], 1)
 
     return np.concatenate([*wide(blocks), *wide(tokens)], 0).astype(np.float32)
+
+
+def chunk_bounds(depth):
+    edges = [depth * eighths // 8 for eighths in (0, 1, 3, 5, 7, 8)]
+    return list(zip(edges[:-1], edges[1:], strict=True))
+
+
+def far_first(engines):
+    side = max(1, round(math.sqrt(engines // 2)))
+    if side * side * 2 != engines:
+        return [(0, 0, 0, i) for i in range(1, engines)]
+    steps = [(x, y, c) for x in range(side) for y in range(side) for c in range(2)][1:]
+    hops = lambda p: 2 * (min(p[0], side - p[0]) + min(p[1], side - p[1])) + p[2]
+    return [(side, *p) for p in sorted(steps, key=hops, reverse=True)]
 
 
 def dot(a, b):
@@ -119,12 +133,22 @@
     sem_w,
     sem_r,
     sem_s,
+    here,
     sem_f,
     sem_q,
     sem_p,
 ):
     me = lax.axis_index("engine")
     z = lax.axis_index("tp")
+    order = far_first(engines)
+
+    def partner(step):
+        side, dx, dy, dc = step
+        if side == 0:
+            return lax.rem(me + dc, engines)
+        x, y, core = me // (2 * side), me // 2 % side, me % 2
+        return (lax.rem(x + dx, side) * side + lax.rem(y + dy, side)) * 2 + lax.rem(core + dc, 2)
+
     width = wk.shape[1]
     depth = wk.shape[0]
     heads = width // HD
@@ -132,15 +156,15 @@
     pairs = engines * sh
     inner = sh * rows
     tokens = sends * SPAN
-    chunks = sem_x.shape[0]
-    chunk = depth // chunks
+    bounds = chunk_bounds(depth)
+    chunks = len(bounds)
 
     def x_copy(c):
-        part = pl.ds(c * chunk, chunk)
+        part = pl.ds(bounds[c][0], bounds[c][1] - bounds[c][0])
         return pltpu.make_async_copy(x_hbm.at[:, part], xv.at[:, part], sem_x.at[c])
 
     def w_copy(m, c):
-        part = pl.ds(c * chunk, chunk)
+        part = pl.ds(bounds[c][0], bounds[c][1] - bounds[c][0])
         source, target = ((wk_hbm, wk), (wv_hbm, wv))[m]
         return pltpu.make_async_copy(source.at[part], target.at[part], sem_w.at[m, c])
 
@@ -161,51 +185,62 @@
             )
         )
     ]
-    x_copy(0).start()
-    for copy in small[:5]:
+    for copy in small:
         copy.start()
-    for c in range(chunks):
+
+    def start_chunk(c):
+        x_copy(c).start()
         w_copy(0, c).start()
         w_copy(1, c).start()
-        if c + 1 < chunks:
-            x_copy(c + 1).start()
-        if c == 0:
-            for copy in small[5:]:
-                copy.start()
+
+    start_chunk(0)
+
+    barrier = pltpu.get_barrier_semaphore()
+
+    for step in order:
+        pl.semaphore_signal(
+            barrier, inc=1, device_id=(partner(step), z), device_id_type=MESH
+        )
+
+    def greet_higher(other, carry):
+        pl.semaphore_signal(barrier, inc=1, device_id=(me, other), device_id_type=MESH)
+        return carry
+
+    lax.fori_loop(z + 1, tps, greet_higher, 0)
+
+    for c in range(1, chunks):
+        start_chunk(c)
     rk_copy = pltpu.make_async_copy(rk_hbm, rk, sem_r.at[0])
     rv_copy = pltpu.make_async_copy(rv_hbm, rv, sem_r.at[1])
     rk_copy.start()
     rv_copy.start()
 
-    barrier = pltpu.get_barrier_semaphore()
-
-    def greet_engine(i, carry):
-        other = lax.rem(me + i, engines)
-        pl.semaphore_signal(barrier, inc=1, device_id=(other, z), device_id_type=MESH)
-        return carry
-
-    def greet_tp(i, carry):
-        other = lax.rem(z + i, tps)
-        pl.semaphore_signal(barrier, inc=1, device_id=(me, other), device_id_type=MESH)
-        return carry
-
-    lax.fori_loop(1, engines, greet_engine, 0)
-    lax.fori_loop(1, tps, greet_tp, 0)
-
-    small[0].wait()
-    small[1].wait()
-    fw = depth // 8
-    fresh = fresh_v[...].astype(F32)
-    fresh = fresh * lax.rsqrt(jnp.mean(fresh * fresh, axis=1, keepdims=True) + NORM_EPS)
-    fresh = fresh * gain_v[...]
-    for s in range(steps):
-        for c in range(8):
-            fst32[s * 8 + c : s * 8 + c + 1, :] = fresh[s : s + 1, c * fw : (c + 1) * fw]
-    fst[...] = fst32[...].astype(BF16)
-    fin[z] = fst[...]
-
-    for copy in small[2:5]:
+    def turn(raw, cosine, sine):
+        return raw * cosine + pltpu.roll(raw, HALF, 1) * sine
+
+    def prepare(c):
+        for j in range(bounds[c][0] // HD, bounds[c][1] // HD):
+            lanes = slice(j * HD, (j + 1) * HD)
+            block = xv[:, lanes].astype(F32)
+            nv[:, lanes] = (block * gain_v[j : j + 1, :]).astype(BF16)
+            square = block * block
+            folded = square if j == bounds[c][0] // HD else folded + square
+        squares[...] = folded if c == 0 else squares[...] + folded
+
+    def multiply(c):
+        part = slice(*bounds[c])
+        for weight, total in ((wk, ak), (wv, av)):
+            raw = dot(nv[:, part], weight[part, :])
+            total[...] = raw if c == 0 else total[...] + raw
+
+    def wait_chunk(c):
+        x_copy(c).wait()
+        w_copy(0, c).wait()
+        w_copy(1, c).wait()
+
+    for copy in small:
         copy.wait()
+
     q = q_v[...].astype(F32)
     q64 = jnp.concatenate(
         [q[s][:, h * HD : (h + 1) * HD] for s in range(steps) for h in range(heads)], axis=0
@@ -238,8 +273,64 @@
     qob[...] = qout.reshape(engines, sh, HD)
     qib[me] = jnp.zeros((sh, HD), F32)
 
-    for copy in small[5:]:
-        copy.wait()
+
+    def q_copy(step):
+        other = partner(step)
+        return pltpu.make_async_remote_copy(
+            src_ref=qob.at[other],
+            dst_ref=qib.at[me],
+            send_sem=sem_q.at[0],
+            recv_sem=sem_q.at[1],
+            device_id=(other, z),
+            device_id_type=MESH,
+        )
+
+    pl.semaphore_wait(barrier, engines - 1 + z)
+    for step in order:
+        q_copy(step).start()
+
+    fw = depth // 8
+    fresh = fresh_v[...].astype(F32)
+    fresh = fresh * lax.rsqrt(jnp.mean(fresh * fresh, axis=1, keepdims=True) + NORM_EPS)
+    for s in range(steps):
+        for j in range(depth // HD):
+            row, at = s * 8 + j * HD // fw, j * HD % fw
+            fst32[row : row + 1, at : at + HD] = (
+                fresh[s : s + 1, j * HD : (j + 1) * HD] * gain_v[j : j + 1, :]
+            )
+    fst[...] = fst32[...].astype(BF16)
+    fin[z] = fst[...]
+
+
+    def f_copy(other):
+        return pltpu.make_async_remote_copy(
+            src_ref=fst,
+            dst_ref=fin.at[z],
+            send_sem=sem_f.at[0],
+            recv_sem=sem_f.at[1],
+            device_id=(me, other),
+            device_id_type=MESH,
+        )
+
+    def answer_lower(other, carry):
+        pl.semaphore_signal(here, inc=1, device_id=(me, other), device_id_type=MESH)
+        f_copy(other).start()
+        return carry
+
+    def send_higher(other, carry):
+        f_copy(other).start()
+        return carry
+
+    lax.fori_loop(0, z, answer_lower, 0)
+
+    wait_chunk(0)
+    prepare(0)
+    multiply(0)
+
+    wait_chunk(1)
+    prepare(1)
+    multiply(1)
+
     nb = CTX // SPAN + 8
     tok_cos = tab_v[2 * nb : 2 * nb + SPAN, :]
     tok_sin = tab_v[2 * nb + SPAN : 2 * nb + 2 * SPAN, :]
@@ -255,73 +346,18 @@
     oi, ol = iota((pairs, sends * sh), 0), iota((pairs, sends * sh), 1)
     place[...] = jnp.where((lane_target == oi // sh) & (oi % sh == ol % sh), 1.0, 0.0).astype(BF16)
 
-    def q_copy(i):
-        other = lax.rem(me + i, engines)
-        return pltpu.make_async_remote_copy(
-            src_ref=qob.at[other],
-            dst_ref=qib.at[me],
-            send_sem=sem_q.at[0],
-            recv_sem=sem_q.at[1],
-            device_id=(other, z),
-            device_id_type=MESH,
-        )
-
-    def f_copy(i):
-        other = lax.rem(z + i, tps)
-        return pltpu.make_async_remote_copy(
-            src_ref=fst,
-            dst_ref=fin.at[z],
-            send_sem=sem_f.at[0],
-            recv_sem=sem_f.at[1],
-            device_id=(me, other),
-            device_id_type=MESH,
-        )
-
-    def start_q(i, carry):
-        q_copy(i).start()
-        return carry
-
-    def start_f(i, carry):
-        f_copy(i).start()
-        return carry
-
-    def turn(raw, cosine, sine):
-        return raw * cosine + pltpu.roll(raw, HALF, 1) * sine
-
-    for c in range(chunks):
-        part = slice(c * chunk, (c + 1) * chunk)
-        x_copy(c).wait()
-        block = xv[:, part].astype(F32)
-        nv[:, part] = (block * gain_v[:, part]).astype(BF16)
-        sq = block * block
-        folded = sum(sq[:, j * HD : (j + 1) * HD] for j in range(chunk // HD))
-        squares[...] = folded if c == 0 else squares[...] + folded
-        last = c == chunks - 1
-        if last:
-            mean = jnp.sum(squares[...], axis=1, keepdims=True) * (1.0 / depth)
-            factor = lax.rsqrt(mean + NORM_EPS)
-            cosv[...] = cosv[...] * factor
-            sinv[...] = sinv[...] * factor
-        w_copy(0, c).wait()
-        raw = dot(nv[:, part], wk[part, :])
-        raw = raw if c == 0 else ak[...] + raw
-        if last:
-            for h in range(heads):
-                head = slice(h * HD, (h + 1) * HD)
-                kb[:, head] = turn(raw[:, head], cosv[...], sinv[...]).astype(BF16)
-        else:
-            ak[...] = raw
-        w_copy(1, c).wait()
-        raw = dot(nv[:, part], wv[part, :])
-        raw = raw if c == 0 else av[...] + raw
-        if last:
-            vb[...] = (raw * factor).astype(BF16)
-        else:
-            av[...] = raw
-        if c == chunks // 2 - 1:
-            pl.semaphore_wait(barrier, engines - 1 + tps - 1)
-            lax.fori_loop(1, engines, start_q, 0)
-            lax.fori_loop(1, tps, start_f, 0)
+    for c in range(2, chunks):
+        wait_chunk(c)
+        prepare(c)
+        multiply(c)
+    mean = jnp.sum(squares[...], axis=1, keepdims=True) * (1.0 / depth)
+    factor = lax.rsqrt(mean + NORM_EPS)
+    cosine = cosv[...] * factor
+    sine = sinv[...] * factor
+    for h in range(heads):
+        head = slice(h * HD, (h + 1) * HD)
+        kb[:, head] = turn(ak[:, head], cosine, sine).astype(BF16)
+    vb[...] = (av[...] * factor).astype(BF16)
 
     scale = 1.0 / math.sqrt(HD)
     everyone = pltpu.make_async_remote_copy(
@@ -363,8 +399,8 @@
         [placed[:, :HD].reshape(engines, sh, HD), placed[:, HD:].reshape(engines, sh, HD)], axis=1
     ).astype(BF16)
 
-    def p_copy(i):
-        other = lax.rem(me + i, engines)
+    def p_copy(step):
+        other = partner(step)
         return pltpu.make_async_remote_copy(
             src_ref=pob.at[other],
             dst_ref=pib.at[me],
@@ -374,12 +410,15 @@
             device_id_type=MESH,
         )
 
-    def start_p(i, carry):
-        p_copy(i).start()
-        return carry
-
-    lax.fori_loop(1, engines, start_p, 0)
+    for step in order:
+        p_copy(step).start()
     pib[me] = jnp.zeros((2 * sh, HD), BF16)
+
+    @pl.when(z < tps - 1)
+    def _():
+        pl.semaphore_wait(here, tps - 1 - z)
+
+    lax.fori_loop(z + 1, tps, send_higher, 0)
 
     fresh_all = pltpu.make_async_remote_copy(
         src_ref=fin.at[pl.ds(0, tps - 1)],
@@ -506,7 +545,7 @@
     tokens = sends * span
     vmem = pl.BlockSpec(memory_space=pltpu.VMEM)
     hbm = pl.BlockSpec(memory_space=pltpu.HBM)
-    chunks = 8
+    chunks = len(chunk_bounds(depth))
     table = jnp.asarray(rope_tables(steps))
     return pl.pallas_call(
         functools.partial(kernel, engines, tps, sends, rows, steps),
@@ -541,7 +580,7 @@
             pltpu.SMEM((rows,), jnp.int32),
             pltpu.VMEM((sends, engines), jnp.int32),
             pltpu.VMEM((sends, engines), jnp.int32),
-            pltpu.VMEM((1, depth), F32),
+            pltpu.VMEM((depth // HD, HD), F32),
             pltpu.VMEM(table.shape, F32),
             pltpu.VMEM((steps, depth), BF16),
             pltpu.VMEM((steps, rows, width), BF16),
@@ -549,6 +588,7 @@
             pltpu.SemaphoreType.DMA((2, chunks)),
             pltpu.SemaphoreType.DMA((2,)),
             pltpu.SemaphoreType.DMA((10,)),
+            pltpu.SemaphoreType.REGULAR,
             pltpu.SemaphoreType.DMA((2,)),
             pltpu.SemaphoreType.DMA((2,)),
             pltpu.SemaphoreType.DMA((2,)),
@@ -563,7 +603,7 @@
         span_block.T,
         span_tokens.T,
         res_len,
-        norm_gain.reshape(1, depth),
+        norm_gain.reshape(depth // HD, HD),
         table,
         fresh_states.reshape(steps, depth),
         queries,

time: 24.9 us -> 21.4 us (0.86)
  the two profiles are of different devices: /device:TPU:1 before, /device:TPU:225 now
where the time goes in v3:
time: 21.4 us; the launch traced here: 21.2 us
  Pallas kernels  19.8 us (93%)
  local copies, waits for them, and re-layouts  1.32 us (6%)
    pallas_call x1, Pallas kernels, per_device(): pl.pallas_call(functools.partial(kernel, engines, tps, sends, rows, steps...  19.8 us
    unnamed x1, local copies, waits for them, and re-layouts  1.32 us

profile of v3, /device:TPU:225, one launch (start us, length us, event | category | flops | bytes accessed | tf_op | source)
XLA Modules:
  0.0 21.2 jit_solution(6490562515090220165)
XLA Ops:
  0.0 19.8 %shard_map.136 = bf16[2,8,512]{2,1,0:T(8,128)(2,1)} custom-call(bf16[384,4096]{1,0:T(8,128)(2,1)} %bitcast.9, s32[12,32]{1,0:T(8,128)} %bitcast.14, s32[12,32]{1,0:T(8,128)} %bitcast.15, s32[12,32]{1,0:T(8,128)} %bitcast.16, s32[12,32]{1,0:T(8,128)} %bitcast.17, s32[8]{0:T(128)} %len_hbm.1, f32[32,128]{1,0:T(8,128)} %bitcast.12, ...), custom_call_target="tpu_custom_call" | custom-call | tf_op jit(solution)/shard_map/pallas_call | solution.py:550
  19.9 1.3 %copy.16 = bf16[2,8,512]{2,1,0:T(8,128)(2,1)} copy(bf16[2,8,512]{2,1,0:T(8,128)(2,1)} %shard_map.136) | data formatting | bytes 32768

commit v4 on v3

--- a/solution.py
+++ b/solution.py
@@ -168,15 +168,27 @@
         source, target = ((wk_hbm, wk), (wv_hbm, wv))[m]
         return pltpu.make_async_copy(source.at[part], target.at[part], sem_w.at[m, c])
 
+    barrier = pltpu.get_barrier_semaphore()
+    for step in order:
+        pl.semaphore_signal(
+            barrier, inc=1, device_id=(partner(step), z), device_id_type=MESH
+        )
+
+    def greet_higher(other, carry):
+        pl.semaphore_signal(barrier, inc=1, device_id=(me, other), device_id_type=MESH)
+        return carry
+
+    lax.fori_loop(z + 1, tps, greet_higher, 0)
+
     small = [
         pltpu.make_async_copy(source, target, sem_s.at[i])
         for i, (source, target) in enumerate(
             (
-                (gain_hbm, gain_v),
-                (fresh_hbm, fresh_v),
                 (q_hbm, q_v),
                 (tgt_hbm, tgt_v),
                 (row_hbm, row_v),
+                (gain_hbm, gain_v),
+                (fresh_hbm, fresh_v),
                 (tgt_hbm, tgt_s),
                 (blk_hbm, blk_s),
                 (tok_hbm, tok_s),
@@ -195,26 +207,6 @@
 
     start_chunk(0)
 
-    barrier = pltpu.get_barrier_semaphore()
-
-    for step in order:
-        pl.semaphore_signal(
-            barrier, inc=1, device_id=(partner(step), z), device_id_type=MESH
-        )
-
-    def greet_higher(other, carry):
-        pl.semaphore_signal(barrier, inc=1, device_id=(me, other), device_id_type=MESH)
-        return carry
-
-    lax.fori_loop(z + 1, tps, greet_higher, 0)
-
-    for c in range(1, chunks):
-        start_chunk(c)
-    rk_copy = pltpu.make_async_copy(rk_hbm, rk, sem_r.at[0])
-    rv_copy = pltpu.make_async_copy(rv_hbm, rv, sem_r.at[1])
-    rk_copy.start()
-    rv_copy.start()
-
     def turn(raw, cosine, sine):
         return raw * cosine + pltpu.roll(raw, HALF, 1) * sine
 
@@ -238,9 +230,8 @@
         w_copy(0, c).wait()
         w_copy(1, c).wait()
 
-    for copy in small:
+    for copy in small[:3]:
         copy.wait()
-
     q = q_v[...].astype(F32)
     q64 = jnp.concatenate(
         [q[s][:, h * HD : (h + 1) * HD] for s in range(steps) for h in range(heads)], axis=0
@@ -285,9 +276,21 @@
             device_id_type=MESH,
         )
 
-    pl.semaphore_wait(barrier, engines - 1 + z)
-    for step in order:
-        q_copy(step).start()
+    for c in range(1, chunks):
+        start_chunk(c)
+    rk_copy = pltpu.make_async_copy(rk_hbm, rk, sem_r.at[0])
+    rv_copy = pltpu.make_async_copy(rv_hbm, rv, sem_r.at[1])
+    rk_copy.start()
+    rv_copy.start()
+
+
+    small[3].wait()
+    wait_chunk(0)
+    prepare(0)
+    multiply(0)
+
+    for copy in small[4:]:
+        copy.wait()
 
     fw = depth // 8
     fresh = fresh_v[...].astype(F32)
@@ -321,11 +324,10 @@
         f_copy(other).start()
         return carry
 
+    pl.semaphore_wait(barrier, engines - 1 + z)
     lax.fori_loop(0, z, answer_lower, 0)
-
-    wait_chunk(0)
-    prepare(0)
-    multiply(0)
+    for step in order:
+        q_copy(step).start()
 
     wait_chunk(1)
     prepare(1)
@@ -368,6 +370,18 @@
         device_id=(me, z),
         device_id_type=MESH,
     )
+
+    def reach_higher():
+        @pl.when(z < tps - 1)
+        def _():
+            pl.semaphore_wait(here, tps - 1 - z)
+
+        lax.fori_loop(z + 1, tps, send_higher, 0)
+
+    @pl.when(z >= tps // 2)
+    def _():
+        reach_higher()
+
     everyone.wait_recv()
     made = []
     for g in range(0, sends, HD // SPAN):
@@ -414,42 +428,9 @@
         p_copy(step).start()
     pib[me] = jnp.zeros((2 * sh, HD), BF16)
 
-    @pl.when(z < tps - 1)
+    @pl.when(z < tps // 2)
     def _():
-        pl.semaphore_wait(here, tps - 1 - z)
-
-    lax.fori_loop(z + 1, tps, send_higher, 0)
-
-    fresh_all = pltpu.make_async_remote_copy(
-        src_ref=fin.at[pl.ds(0, tps - 1)],
-        dst_ref=fin.at[pl.ds(0, tps - 1)],
-        send_sem=sem_f.at[0],
-        recv_sem=sem_f.at[1],
-        device_id=(me, z),
-        device_id_type=MESH,
-    )
-    fresh_all.wait_recv()
-    fr = rows * steps * 8
-    ri, rl = iota((fr, fr), 0), iota((fr, fr), 1)
-    want = (ri % rows) * (steps * 8) + (ri // rows % steps) * 8 + ri // (rows * steps)
-    order = jnp.where(rl == want, 1.0, 0.0).astype(BF16)
-    sorted_fresh = dot(order, fin[...].reshape(fr, fw)).astype(BF16)
-    new = rows * steps
-    fn = jnp.concatenate(
-        [sorted_fresh[c * new : (c + 1) * new, :] for c in range(8)], axis=1
-    )
-    f_step = iota((new, 1), 0) // rows
-    f_cos = jnp.zeros((new, HD), F32)
-    f_sin = jnp.zeros((new, HD), F32)
-    bc = CTX // SPAN
-    for t in range(steps):
-        c0, s0 = tab_v[bc : bc + 1, :], tab_v[nb + bc : nb + bc + 1, :]
-        c1, s1 = tok_cos[t : t + 1, :], tok_sin[t : t + 1, :]
-        f_cos = jnp.where(f_step == t, c0 * c1 - s0 * s1, f_cos)
-        f_sin = jnp.where(f_step == t, s0 * c1 + c0 * s1, f_sin)
-    raw = dot(fn, wk[...])
-    fk = jnp.concatenate([turn(b, f_cos, f_sin) for b in per_head(raw, heads)], axis=1).astype(BF16)
-    fv = dot(fn, wv[...]).astype(BF16)
+        reach_higher()
 
     near = rk.shape[0]
     resident = near // rows
@@ -464,19 +445,51 @@
         ok = (lane_near >= r * resident) & (lane_near < r * resident + len_s[r])
         col_row = jnp.where(ok, r, col_row)
     live_near = col_row == in_row % rows
+    s_near = jnp.where(live_near, dot_nt(q_near, rk[...]) * scale, NEG)
+    peak_near = jnp.max(s_near, axis=1, keepdims=True)
+    p_near = jnp.where(live_near, jnp.exp(s_near - peak_near), 0.0)
+    total_near = jnp.sum(p_near, axis=1, keepdims=True)
+    sum_near = own_head(dot(p_near.astype(BF16), rv[...]), heads, in_head)
+
+    fresh_all = pltpu.make_async_remote_copy(
+        src_ref=fin.at[pl.ds(0, tps - 1)],
+        dst_ref=fin.at[pl.ds(0, tps - 1)],
+        send_sem=sem_f.at[0],
+        recv_sem=sem_f.at[1],
+        device_id=(me, z),
+        device_id_type=MESH,
+    )
+    fresh_all.wait_recv()
+    fr = rows * steps * 8
+    ri, rl = iota((fr, fr), 0), iota((fr, fr), 1)
+    want = (ri % rows) * (steps * 8) + (ri // rows % steps) * 8 + ri // (rows * steps)
+    order = jnp.where(rl == want, 1.0, 0.0).astype(BF16)
+    sorted_fresh = dot(order, fin[...].reshape(fr, fw)).astype(BF16)
+    new = rows * steps
+    fn = jnp.concatenate(
+        [sorted_fresh[c * new : (c + 1) * new, :] for c in range(8)], axis=1
+    )
+    f_step = iota((new, 1), 0) // rows
+    f_cos = jnp.zeros((new, HD), F32)
+    f_sin = jnp.zeros((new, HD), F32)
+    bc = CTX // SPAN
+    for t in range(steps):
+        c0, s0 = tab_v[bc : bc + 1, :], tab_v[nb + bc : nb + bc + 1, :]
+        c1, s1 = tok_cos[t : t + 1, :], tok_sin[t : t + 1, :]
+        f_cos = jnp.where(f_step == t, c0 * c1 - s0 * s1, f_cos)
+        f_sin = jnp.where(f_step == t, s0 * c1 + c0 * s1, f_sin)
+    raw = dot(fn, wk[...])
+    fk = jnp.concatenate([turn(b, f_cos, f_sin) for b in per_head(raw, heads)], axis=1).astype(BF16)
+    fv = dot(fn, wv[...]).astype(BF16)
+
     lane_new = iota((1, new), 1)
     live_new = (lane_new % rows == in_row % rows) & (lane_new // rows <= in_row // (rows * heads))
-    s_near = jnp.where(live_near, dot_nt(q_near, rk[...]) * scale, NEG)
     s_new = jnp.where(live_new, dot_nt(q_near, fk) * scale, NEG)
-    peak_n = jnp.maximum(
-        jnp.max(s_near, axis=1, keepdims=True), jnp.max(s_new, axis=1, keepdims=True)
-    )
-    p_near = jnp.where(live_near, jnp.exp(s_near - peak_n), 0.0)
+    peak_n = jnp.maximum(peak_near, jnp.max(s_new, axis=1, keepdims=True))
     p_new = jnp.where(live_new, jnp.exp(s_new - peak_n), 0.0)
-    total_n = jnp.sum(p_near, axis=1, keepdims=True) + jnp.sum(p_new, axis=1, keepdims=True)
-    o_near = own_head(
-        dot(p_near.astype(BF16), rv[...]) + dot(p_new.astype(BF16), fv), heads, in_head
-    )
+    keep = jnp.exp(peak_near - peak_n)
+    total_n = keep * total_near + jnp.sum(p_new, axis=1, keepdims=True)
+    o_near = keep * sum_near + own_head(dot(p_new.astype(BF16), fv), heads, in_head)
 
     from_all = pltpu.make_async_remote_copy(
         src_ref=pob.at[pl.ds(0, engines - 1)],
@@ -489,19 +502,21 @@
     from_all.wait_recv()
     pin = pib[...].astype(F32)
     o_in = pin[:, :sh, :].reshape(pairs, HD)
-    parts = pin[:, sh:, :].reshape(pairs, HD)
-    lse_in = parts[:, 0:1] + parts[:, 32:33] + parts[:, 64:65]
+    parts = pin[:, sh:, :].reshape(pairs, HD).astype(BF16)
+    third = iota((HD, HD), 0)
+    add_up = jnp.where((third == 0) | (third == 32) | (third == 64), 1.0, 0.0).astype(BF16)
+    lse_in = dot(parts, add_up)
     eye = iota((inner, inner), 0) == iota((inner, inner), 1)
     peak_lane = jnp.sum(jnp.where(eye, peak_n, 0.0), axis=0, keepdims=True)
     top = jnp.maximum(
-        jnp.max(jnp.where(pick, lse_in, NEG), axis=0, keepdims=True), peak_lane
+        jnp.max(jnp.where(pick, lse_in[:, :inner], NEG), axis=0, keepdims=True), peak_lane
     )
     top_pair = jnp.sum(jnp.where(pick, top, 0.0), axis=1, keepdims=True)
     top_in = jnp.sum(jnp.where(eye, top, 0.0), axis=1, keepdims=True)
     valid = row_col > 0.0
     w_in = jnp.where(valid, jnp.exp(jnp.where(valid, lse_in - top_pair, 0.0)), 0.0)
     weighted = jnp.concatenate(
-        [jnp.where(valid, w_in * o_in, 0.0), jnp.broadcast_to(w_in, (pairs, HD))], axis=1
+        [jnp.where(valid, w_in * o_in, 0.0), w_in], axis=1
     )
     first = weighted.astype(BF16)
     second = (weighted - first.astype(F32)).astype(BF16)

time: 21.4 us -> 20.4 us (0.953)
  the two profiles are of different devices: /device:TPU:225 before, /device:TPU:1 now
where the time goes in v4:
time: 20.4 us; the launch traced here: 20.1 us
  Pallas kernels  18.8 us (92%)
  local copies, waits for them, and re-layouts  1.32 us (6%)
    pallas_call x1, Pallas kernels, per_device(): pl.pallas_call(functools.partial(kernel, engines, tps, sends, rows, steps...  18.8 us
    unnamed x1, local copies, waits for them, and re-layouts  1.32 us

profile of v4, /device:TPU:1, one launch (start us, length us, event | category | flops | bytes accessed | tf_op | source)
XLA Modules:
  0.0 20.1 jit_solution(1955020817127541806)
XLA Ops:
  0.0 18.8 %shard_map.136 = bf16[2,8,512]{2,1,0:T(8,128)(2,1)} custom-call(bf16[384,4096]{1,0:T(8,128)(2,1)} %bitcast.9, s32[12,32]{1,0:T(8,128)} %bitcast.14, s32[12,32]{1,0:T(8,128)} %bitcast.15, s32[12,32]{1,0:T(8,128)} %bitcast.16, s32[12,32]{1,0:T(8,128)} %bitcast.17, s32[8]{0:T(128)} %len_hbm.1, f32[32,128]{1,0:T(8,128)} %bitcast.12, ...), custom_call_target="tpu_custom_call" | custom-call | tf_op jit(solution)/shard_map/pallas_call | solution.py:565
  18.8 1.3 %copy.16 = bf16[2,8,512]{2,1,0:T(8,128)(2,1)} copy(bf16[2,8,512]{2,1,0:T(8,128)(2,1)} %shard_map.136) | data formatting | bytes 32768

commit v5 on v4

--- a/solution.py
+++ b/solution.py
@@ -119,6 +119,8 @@
     pob,
     pib,
     place,
+    collect_v,
+    add_v,
     tgt_s,
     blk_s,
     tok_s,
@@ -261,8 +263,8 @@
     ti, tl = iota((inner, pairs), 0), iota((inner, pairs), 1)
     pick_t = (row_lane == (ti % rows + 1).astype(F32)) & (tl % sh == ti // rows)
     qout = dot(jnp.where(pick, 1.0, 0.0).astype(BF16), q64.astype(BF16))
-    qob[...] = qout.reshape(engines, sh, HD)
-    qib[me] = jnp.zeros((sh, HD), F32)
+    qob[...] = qout.reshape(engines, sh, HD).astype(BF16)
+    qib[me] = jnp.zeros((sh, HD), BF16)
 
 
     def q_copy(step):
@@ -359,7 +361,6 @@
     for h in range(heads):
         head = slice(h * HD, (h + 1) * HD)
         kb[:, head] = turn(ak[:, head], cosine, sine).astype(BF16)
-    vb[...] = (av[...] * factor).astype(BF16)
 
     scale = 1.0 / math.sqrt(HD)
     everyone = pltpu.make_async_remote_copy(
@@ -383,12 +384,13 @@
         reach_higher()
 
     everyone.wait_recv()
+    vb[...] = (av[...] * factor).astype(BF16)
     made = []
     for g in range(0, sends, HD // SPAN):
         spans = range(g, min(g + HD // SPAN, sends))
         count = len(spans)
         group = slice(g * SPAN, (g + count) * SPAN)
-        q_g = jnp.concatenate([qib[tgt_s[k, me]] for k in spans], axis=0)
+        q_g = jnp.concatenate([qib[tgt_s[k, me]].astype(F32) for k in spans], axis=0)
         g_row = iota((count * sh, 1), 0)
         g_lane = iota((1, count * SPAN), 1)
         edge = jnp.zeros((count * sh, 1), jnp.int32)
@@ -491,6 +493,12 @@
     total_n = keep * total_near + jnp.sum(p_new, axis=1, keepdims=True)
     o_near = keep * sum_near + own_head(dot(p_new.astype(BF16), fv), heads, in_head)
 
+    third = iota((HD, HD), 0)
+    add_up = jnp.where((third == 0) | (third == 32) | (third == 64), 1.0, 0.0).astype(BF16)
+    eye = iota((inner, inner), 0) == iota((inner, inner), 1)
+    peak_lane = jnp.sum(jnp.where(eye, peak_n, 0.0), axis=0, keepdims=True)
+    collect_v[...] = jnp.where(pick_t, 1.0, 0.0).astype(BF16)
+    add_v[...] = add_up
     from_all = pltpu.make_async_remote_copy(
         src_ref=pob.at[pl.ds(0, engines - 1)],
         dst_ref=pib.at[pl.ds(0, engines - 1)],
@@ -503,11 +511,7 @@
     pin = pib[...].astype(F32)
     o_in = pin[:, :sh, :].reshape(pairs, HD)
     parts = pin[:, sh:, :].reshape(pairs, HD).astype(BF16)
-    third = iota((HD, HD), 0)
-    add_up = jnp.where((third == 0) | (third == 32) | (third == 64), 1.0, 0.0).astype(BF16)
-    lse_in = dot(parts, add_up)
-    eye = iota((inner, inner), 0) == iota((inner, inner), 1)
-    peak_lane = jnp.sum(jnp.where(eye, peak_n, 0.0), axis=0, keepdims=True)
+    lse_in = dot(parts, add_v[...])
     top = jnp.maximum(
         jnp.max(jnp.where(pick, lse_in[:, :inner], NEG), axis=0, keepdims=True), peak_lane
     )
@@ -520,8 +524,7 @@
     )
     first = weighted.astype(BF16)
     second = (weighted - first.astype(F32)).astype(BF16)
-    collect = jnp.where(pick_t, 1.0, 0.0).astype(BF16)
-    gathered = dot(collect, first) + dot(collect, second)
+    gathered = dot(collect_v[...], first) + dot(collect_v[...], second)
     w_near = jnp.exp(peak_n - top_in)
     result = (w_near * o_near + gathered[:, :HD]) / (w_near * total_n + gathered[:, HD:])
     for t in range(steps):
@@ -584,11 +587,13 @@
             pltpu.VMEM((steps * 8, depth // 8), F32),
             pltpu.VMEM((steps * 8, depth // 8), BF16),
             pltpu.VMEM((tps, steps * 8, depth // 8), BF16),
-            pltpu.VMEM((engines, sh, HD), F32),
-            pltpu.VMEM((engines, sh, HD), F32),
+            pltpu.VMEM((engines, sh, HD), BF16),
+            pltpu.VMEM((engines, sh, HD), BF16),
             pltpu.VMEM((engines, 2 * sh, HD), BF16),
             pltpu.VMEM((engines, 2 * sh, HD), BF16),
             pltpu.VMEM((engines * sh, sends * sh), BF16),
+            pltpu.VMEM((sh * rows, engines * sh), BF16),
+            pltpu.VMEM((HD, HD), BF16),
             pltpu.SMEM((sends, engines), jnp.int32),
             pltpu.SMEM((sends, engines), jnp.int32),
             pltpu.SMEM((sends, engines), jnp.int32),

time: 20.4 us -> 20.1 us (0.985)
  Pallas kernels: 18.8 us -> 18.5 us
    pallas_call x1, Pallas kernels: 18.8 us -> 18.5 us  [per_device(): pl.pallas_call(functools.partial(kernel, engines, tps, sends, rows, steps...]
where the time goes in v5:
time: 20.1 us; the launch traced here: 19.8 us
  Pallas kernels  18.5 us (92%)
  local copies, waits for them, and re-layouts  1.32 us (7%)
    pallas_call x1, Pallas kernels, per_device(): pl.pallas_call(functools.partial(kernel, engines, tps, sends, rows, steps...  18.5 us
    unnamed x1, local copies, waits for them, and re-layouts  1.32 us

profile of v5, /device:TPU:1, one launch (start us, length us, event | category | flops | bytes accessed | tf_op | source)
XLA Modules:
  0.0 19.8 jit_solution(16741531655973825793)
XLA Ops:
  0.0 18.5 %shard_map.136 = bf16[2,8,512]{2,1,0:T(8,128)(2,1)} custom-call(bf16[384,4096]{1,0:T(8,128)(2,1)} %bitcast.9, s32[12,32]{1,0:T(8,128)} %bitcast.14, s32[12,32]{1,0:T(8,128)} %bitcast.15, s32[12,32]{1,0:T(8,128)} %bitcast.16, s32[12,32]{1,0:T(8,128)} %bitcast.17, s32[8]{0:T(128)} %len_hbm.1, f32[32,128]{1,0:T(8,128)} %bitcast.12, ...), custom_call_target="tpu_custom_call" | custom-call | tf_op jit(solution)/shard_map/pallas_call | solution.py:568
  18.5 1.3 %copy.16 = bf16[2,8,512]{2,1,0:T(8,128)(2,1)} copy(bf16[2,8,512]{2,1,0:T(8,128)(2,1)} %shard_map.136) | data formatting | bytes 32768

commit v6 on v5

--- a/solution.py
+++ b/solution.py
@@ -38,7 +38,7 @@
 
 
 def chunk_bounds(depth):
-    edges = [depth * eighths // 8 for eighths in (0, 1, 3, 5, 7, 8)]
+    edges = [depth * eighths // 8 for eighths in (0, 1, 4, 7, 8)]
     return list(zip(edges[:-1], edges[1:], strict=True))
 
 
@@ -144,12 +144,16 @@
     z = lax.axis_index("tp")
     order = far_first(engines)
 
+    side = order[0][0]
+    if side:
+        at_x = [lax.rem(me // (2 * side) + d, side) * (2 * side) for d in range(side)]
+        at_y = [lax.rem(me // 2 % side + d, side) * 2 for d in range(side)]
+        at_core = [lax.rem(me % 2 + d, 2) for d in range(2)]
+
     def partner(step):
-        side, dx, dy, dc = step
         if side == 0:
-            return lax.rem(me + dc, engines)
-        x, y, core = me // (2 * side), me // 2 % side, me % 2
-        return (lax.rem(x + dx, side) * side + lax.rem(y + dy, side)) * 2 + lax.rem(core + dc, 2)
+            return lax.rem(me + step[3], engines)
+        return at_x[step[1]] + at_y[step[2]] + at_core[step[3]]
 
     width = wk.shape[1]
     depth = wk.shape[0]
@@ -169,18 +173,6 @@
         part = pl.ds(bounds[c][0], bounds[c][1] - bounds[c][0])
         source, target = ((wk_hbm, wk), (wv_hbm, wv))[m]
         return pltpu.make_async_copy(source.at[part], target.at[part], sem_w.at[m, c])
-
-    barrier = pltpu.get_barrier_semaphore()
-    for step in order:
-        pl.semaphore_signal(
-            barrier, inc=1, device_id=(partner(step), z), device_id_type=MESH
-        )
-
-    def greet_higher(other, carry):
-        pl.semaphore_signal(barrier, inc=1, device_id=(me, other), device_id_type=MESH)
-        return carry
-
-    lax.fori_loop(z + 1, tps, greet_higher, 0)
 
     small = [
         pltpu.make_async_copy(source, target, sem_s.at[i])
@@ -199,15 +191,31 @@
             )
         )
     ]
-    for copy in small:
-        copy.start()
 
     def start_chunk(c):
         x_copy(c).start()
         w_copy(0, c).start()
         w_copy(1, c).start()
 
+
+    for copy in small[:4]:
+        copy.start()
     start_chunk(0)
+
+    barrier = pltpu.get_barrier_semaphore()
+    for step in order:
+        pl.semaphore_signal(
+            barrier, inc=1, device_id=(partner(step), z), device_id_type=MESH
+        )
+
+    def greet_higher(other, carry):
+        pl.semaphore_signal(barrier, inc=1, device_id=(me, other), device_id_type=MESH)
+        return carry
+
+    lax.fori_loop(z + 1, tps, greet_higher, 0)
+
+    for copy in small[4:]:
+        copy.start()
 
     def turn(raw, cosine, sine):
         return raw * cosine + pltpu.roll(raw, HALF, 1) * sine

time: 20.1 us -> 20 us (level)
  no operation moved by 1% of the time
where the time goes in v6:
time: 20 us; the launch traced here: 19.8 us
  Pallas kernels  18.4 us (92%)
  local copies, waits for them, and re-layouts  1.32 us (7%)
    pallas_call x1, Pallas kernels, per_device(): pl.pallas_call(functools.partial(kernel, engines, tps, sends, rows, steps...  18.4 us
    unnamed x1, local copies, waits for them, and re-layouts  1.32 us

profile of v6, /device:TPU:1, one launch (start us, length us, event | category | flops | bytes accessed | tf_op | source)
XLA Modules:
  0.0 19.8 jit_solution(576382395780048291)
XLA Ops:
  0.0 18.4 %shard_map.136 = bf16[2,8,512]{2,1,0:T(8,128)(2,1)} custom-call(bf16[384,4096]{1,0:T(8,128)(2,1)} %bitcast.9, s32[12,32]{1,0:T(8,128)} %bitcast.14, s32[12,32]{1,0:T(8,128)} %bitcast.15, s32[12,32]{1,0:T(8,128)} %bitcast.16, s32[12,32]{1,0:T(8,128)} %bitcast.17, s32[8]{0:T(128)} %len_hbm.1, f32[32,128]{1,0:T(8,128)} %bitcast.12, ...), custom_call_target="tpu_custom_call" | custom-call | tf_op jit(solution)/shard_map/pallas_call | solution.py:576
  18.4 1.3 %copy.16 = bf16[2,8,512]{2,1,0:T(8,128)(2,1)} copy(bf16[2,8,512]{2,1,0:T(8,128)(2,1)} %shard_map.136) | data formatting | bytes 32768
